TPU v7x, 256 devices: a whole 4x4x8 slice. The times are simulated.
256 devices in a mesh: dp: 16 (over x, y_hi, core), tensor: 16 (over y_lo, z).
Axes of the slice: x: 4, y: 4 (y_hi: 2, y_lo: 2; y = y_hi * 2 + y_lo), z: 8, core: 2. Of those that a mesh axis runs over, the one named last changes fastest.
Arguments:
- inputs: bfloat16 [32768, 5120], P(('dp', 'tensor')), may hold values from -6 to 6
- latent: bfloat16 [32768, 512], P(('dp', 'tensor')), may hold values from -180 to 180
- gain: float32 [512], replicated, may hold values from 0.25 to 1.75
- w_latent: bfloat16 [5120, 512], P('tensor'), may hold values from -0.078125 to 0.078125
- w_rope: bfloat16 [5120, 64], P('tensor'), may hold values from -0.078125 to 0.078125
- w_up: bfloat16 [512, 32768], P('dp', 'tensor'), may hold values from -0.25 to 0.25
- grad_kv: bfloat16 [32768, 32768], P('dp', 'tensor'), may hold values from -6 to 6
- grad_rope: bfloat16 [32768, 64], P(('dp', 'tensor')), may hold values from -6 to 6
Outputs:
- grad_x: bfloat16 [32768, 5120], P(('dp', 'tensor'))
- grad_w_up: bfloat16 [512, 32768], P('dp', 'tensor')
- grad_w_latent: bfloat16 [5120, 512], P('tensor', 'dp')
- grad_w_rope: bfloat16 [5120, 64], P('tensor', 'dp')
- grad_gain: float32 [512], replicated
All inputs are finite; a program needn't handle non-finite values.
Results may differ from a plain program's by a relative error of at most 0.019.
Values may be sent and summed in bfloat16 or wider, within the bound.
A program may use at most 128 MiB of HBM per device.

v0:
```python
import jax
import jax.numpy as jnp
from jax import lax
from jax.sharding import PartitionSpec as P

epsilon = 1e-06


def contract(left, right, left_dim, right_dim):
    return lax.dot_general(
        left, right, (((left_dim,), (right_dim,)), ((), ())), preferred_element_type=jnp.float32
    )


def shards(inputs, latent, gain, w_latent, w_rope, w_up, grad_kv, grad_rope):
    latent_f = latent.astype(jnp.float32)
    inverse = lax.rsqrt(jnp.mean(latent_f * latent_f, axis=-1, keepdims=True) + epsilon)
    normed = (latent_f * inverse * gain).astype(jnp.bfloat16)
    up_full = lax.all_gather(w_up, "dp", axis=0, tiled=True)
    token_rows = grad_kv
    grad_norm = lax.psum_scatter(
        contract(token_rows, up_full, 1, 1), "tensor", scatter_dimension=0, tiled=True
    )
    token_rows = grad_kv
    up_partial = contract(lax.all_gather(normed, "tensor", axis=0, tiled=True), token_rows, 0, 0)
    grad_w_up = lax.psum_scatter(
        up_partial.astype(jnp.bfloat16), "dp", scatter_dimension=0, tiled=True
    )
    scaled = grad_norm * gain
    grad_pre = inverse * scaled - latent_f * inverse**3 * jnp.mean(
        scaled * latent_f, axis=-1, keepdims=True
    )
    grad_pre = grad_pre.astype(jnp.bfloat16)
    gain_part = jnp.sum(grad_norm * latent_f * inverse, axis=0)
    grad_gain = lax.psum(gain_part, ("dp", "tensor"))
    spread = lax.all_to_all(inputs, "tensor", split_axis=1, concat_axis=0, tiled=True)
    full_pre, full_rope = (
        lax.all_gather(grad_pre, "tensor", axis=0, tiled=True),
        lax.all_gather(grad_rope, "tensor", axis=0, tiled=True),
    )
    latent_part = contract(spread, full_pre, 0, 0)
    rope_part = contract(spread, full_rope, 0, 0)
    columns = (contract(full_pre, w_latent, 1, 1) + contract(full_rope, w_rope, 1, 1)).astype(
        jnp.bfloat16
    )
    grad_x = lax.all_to_all(columns, "tensor", split_axis=0, concat_axis=1, tiled=True)
    summed_latent, summed_rope = (
        lax.psum_scatter(latent_part, "dp", scatter_dimension=1, tiled=True),
        lax.psum_scatter(rope_part, "dp", scatter_dimension=1, tiled=True),
    )
    return (
        grad_x,
        grad_w_up,
        summed_latent.astype(jnp.bfloat16),
        summed_rope.astype(jnp.bfloat16),
        grad_gain,
    )


def solution(mesh):
    in_specs = (
        P(("dp", "tensor"), None),
        P(("dp", "tensor"), None),
        P(),
        P("tensor", None),
        P("tensor", None),
        P("dp", "tensor"),
        P("dp", "tensor"),
        P(("dp", "tensor"), None),
    )
    out_specs = (
        P(("dp", "tensor"), None),
        P("dp", "tensor"),
        P("tensor", "dp"),
        P("tensor", "dp"),
        P(),
    )
    return jax.shard_map(shards, mesh=mesh, in_specs=in_specs, out_specs=out_specs, check_vma=False)
```

profile of v0, /device:TPU:1, one launch (start us, length us, event | category | flops | bytes accessed | tf_op | source)
XLA Modules:
  0.0 511.4 jit_solution(17031620215564557166)
XLA Ops:
  7.2 0.0 copy-start
  7.2 0.0 all-gather.4.cloned.1.call-start
  7.2 0.7 all-gather.4.cloned.1.call-update
  7.9 0.0 reduce-scatter.6.cloned.1.call-start
  8.0 60.5 %all-gather.4.cloned.1.call-done = bf16[512,2048]{1,0:T(8,128)(2,1)} async-done(((bf16[32,2048]{1,0:T(8,128)(2,1)}), bf16[512,2048]{1,0:T(8,128)(2,1)}) %all-gather.4.cloned.1.call-update) | async-done | bytes 2097168 | tf_op jit(solution)/shard_map/all_gather | solution.py:19
  68.4 10.5 %fusion.20 = f32[2048,512]{1,0:T(8,128)} fusion(bf16[2048,2048]{1,0:T(8,128)(2,1)} %param.14, bf16[512,2048]{1,0:T(8,128)(2,1)} %all-gather.4.cloned.1.call-done), kind=kOutput, calls=%fused_computation.30 | convolution fusion | flops 4294967296 | bytes 14680064 | tf_op jit(solution)/shard_map/dot_general | solution.py:10
  78.9 0.0 copy-start.5
  78.9 0.0 copy-start.8
  78.9 0.0 copy-start.2
  78.9 0.0 reduce-scatter.6.cloned.1.call-update
  78.9 0.0 all-gather.6.cloned.1.call-start
  79.0 0.8 copy-done.5
  79.8 0.1 fusion.11
  79.9 67.7 %reduce-scatter.6.cloned.1.call-done = f32[128,512]{1,0:T(8,128)} async-done(((f32[2048,512]{1,0:T(8,128)}), f32[128,512]{1,0:T(8,128)}) %reduce-scatter.6.cloned.1.call-update) | async-done | bytes 262160 | tf_op jit(solution)/shard_map/reduce_scatter | solution.py:21
  147.7 0.0 copy-done.8
  147.7 1.1 fusion.19
  148.8 1.8 fusion.17
  150.6 0.0 all-gather.6.cloned.1.call-update
  150.6 0.0 all-gather.8.cloned.1.call-start
  150.7 0.5 all-gather.8.cloned.1.call-update
  151.2 0.0 reduce-scatter.10.cloned.1.call-start
  151.2 0.0 copy-done.2
  151.2 0.8 copy.21
  152.0 25.4 %all_to_all.38 = bf16[128,16,320]{0,2,1:T(8,128)(2,1)S(1)} all-to-all(bf16[128,16,320]{0,2,1:T(8,128)(2,1)S(1)} %bitcast.40), channel_id=1, replica_groups=mesh['dp'=16,'tensor'=16] {'tensor'}, dimensions={1} | all-to-all | bytes 2621440 | tf_op jit(solution)/shard_map/all_to_all | solution.py:36
  177.5 0.0 copy-start.3
  177.5 49.4 %all-gather.6.cloned.1.call-done = bf16[2048,512]{1,0:T(8,128)(2,1)} async-done(((bf16[128,512]{1,0:T(8,128)(2,1)}), bf16[2048,512]{1,0:T(8,128)(2,1)}) %all-gather.6.cloned.1.call-update) | async-done | bytes 2097168 | tf_op jit(solution)/shard_map/all_gather | solution.py:38
  226.9 2.4 fusion.6
  229.3 0.0 copy-done.3
  229.3 1.2 copy.25
  230.6 0.0 reduce-scatter.10.cloned.1.call-update
  230.6 0.0 reduce-scatter.8.cloned.1.call-start
  230.6 64.6 %all-gather.8.cloned.1.call-done = bf16[2048,512]{1,0:T(8,128)(2,1)} async-done(((bf16[128,512]{1,0:T(8,128)(2,1)}), bf16[2048,512]{1,0:T(8,128)(2,1)}) %all-gather.8.cloned.1.call-update) | async-done | bytes 2097168 | tf_op jit(solution)/shard_map/all_gather | solution.py:25
  295.2 0.0 copy-start.7
  295.2 9.9 %convolution_convert_fusion = bf16[512,2048]{1,0:T(8,128)(2,1)} fusion(bf16[2048,512]{1,0:T(8,128)(2,1)} %all-gather.8.cloned.1.call-done, bf16[2048,2048]{1,0:T(8,128)(2,1)} %param.14), kind=kOutput, calls=%fused_computation | convolution fusion | flops 4296015872 | bytes 12582912 | tf_op jit(solution)/shard_map/dot_general | solution.py:10
  305.1 0.0 copy-start.1
  305.1 0.0 reduce-scatter.8.cloned.1.call-update
  305.1 0.0 copy-done.7
  305.1 27.9 %all_gather.14 = bf16[2048,64]{0,1:T(8,128)(2,1)S(1)} all-gather(bf16[128,64]{0,1:T(8,128)(2,1)S(1)} %copy-done.7), channel_id=1, replica_groups=mesh['dp'=16,'tensor'=16] {'tensor'}, dimensions={0}, use_global_device_ids=true | all-gather | bytes 278528 | tf_op jit(solution)/shard_map/all_gather | solution.py:39
  333.0 0.0 copy-done
  333.0 0.0 copy-done.1
  333.0 0.0 copy-start.6
  333.0 0.9 fusion.21
  333.9 0.0 copy-done.6
  333.9 0.5 fusion.1
  334.5 0.0 copy-start.9
  334.5 0.0 copy-start.4
  334.5 1.4 copy.38
  335.9 3.7 all-to-all-start
  339.6 0.0 copy-done.9
  339.6 0.6 dynamic-slice
  340.8 0.0 copy-done.4
  340.8 0.5 fusion.2
  341.4 78.1 %all-reduce = bf16[320,64]{0,1:T(8,128)(2,1)S(1)} all-reduce(f32[320,64]{0,1:T(8,128)S(1)} %fusion.2), channel_id=5, replica_groups=mesh['dp'=16,'tensor'=16] {'dp'}, use_global_device_ids=true, to_apply=%region_5.0.clone | all-reduce | flops 20480 | bytes 122880
  419.4 0.6 dynamic-slice_convert_fusion
  420.0 81.5 %psum.7 = f32[512]{0:T(512)} all-reduce(f32[512]{0:T(512)S(1)} %get-tuple-element.20), channel_id=1, replica_groups=mesh['dp'=16,'tensor'=16] {'dp','tensor'}, use_global_device_ids=true, to_apply=%region_7.0 | all-reduce | flops 512 | bytes 4096 | tf_op jit(solution)/shard_map/psum | solution.py:35
  501.5 0.0 reduce-scatter.10.cloned.1.call-done
  501.5 0.9 copy.26
  502.4 0.7 copy.24
  503.1 0.0 all-to-all-done
  503.1 1.4 copy.23
  504.6 0.0 reduce-scatter.8.cloned.1.call-done
  (2 shorter events, 0.0 us)
Async XLA Ops:
  7.2 325.9 %copy-start = (bf16[320,512]{1,0:T(8,128)(2,1)S(1)}, bf16[320,512]{1,0:T(8,128)(2,1)}, u32[]{:S(2)}) copy-start(bf16[320,512]{1,0:T(8,128)(2,1)} %param.11) | copy-start | bytes 983044
  7.2 61.2 %all-gather.4.cloned.1.call-start = ((), (), s32[]{:S(2)}) async-start(), calls=%async_computation.5 | async-start | bytes 2228224 | tf_op jit(solution)/shard_map/all_gather | solution.py:19
  7.9 139.8 %reduce-scatter.6.cloned.1.call-start = ((), (), s32[]{:S(2)}) async-start(), calls=%async_computation.6 | async-start | bytes 4456448 | tf_op jit(solution)/shard_map/reduce_scatter | solution.py:21
  78.9 0.9 copy-start.5
  78.9 68.8 %copy-start.8 = (f32[512]{0:T(512)S(1)}, f32[512]{0:T(512)}, u32[]{:S(2)}) copy-start(f32[512]{0:T(512)} %param.10) | copy-start | bytes 6148
  78.9 72.3 %copy-start.2 = (bf16[128,5120]{1,0:T(8,128)(2,1)S(1)}, bf16[128,5120]{1,0:T(8,128)(2,1)}, u32[]{:S(2)}) copy-start(bf16[128,5120]{1,0:T(8,128)(2,1)} %param.8) | copy-start | bytes 3932164
  78.9 148.0 %all-gather.6.cloned.1.call-start = ((), (), s32[]{:S(2)}) async-start(), calls=%async_computation.7 | async-start | bytes 2228224 | tf_op jit(solution)/shard_map/all_gather | solution.py:38
  150.6 144.6 %all-gather.8.cloned.1.call-start = ((), (), s32[]{:S(2)}) async-start(), calls=%async_computation.8 | async-start | bytes 2228224 | tf_op jit(solution)/shard_map/all_gather | solution.py:25
  151.2 350.3 %reduce-scatter.10.cloned.1.call-start = ((), (), s32[]{:S(2)}) async-start(), calls=%async_computation.10 | async-start | bytes 835584
  177.5 51.9 %copy-start.3 = (bf16[128,16,320]{0,2,1:T(8,128)(2,1)}, bf16[128,16,320]{0,2,1:T(8,128)(2,1)S(1)}, u32[]{:S(2)}) copy-start(bf16[128,16,320]{0,2,1:T(8,128)(2,1)S(1)} %all_to_all.38) | copy-start | bytes 3932164
  230.6 274.0 %reduce-scatter.8.cloned.1.call-start = ((), (), s32[]{:S(2)}) async-start(), calls=%async_computation.9 | async-start | bytes 2228224 | tf_op jit(solution)/shard_map/reduce_scatter | solution.py:26
  295.2 9.9 %copy-start.7 = (bf16[128,64]{0,1:T(8,128)(2,1)S(1)}, bf16[128,64]{0,1:T(8,128)(2,1)}, u32[]{:S(2)}) copy-start(bf16[128,64]{0,1:T(8,128)(2,1)} %param.15) | copy-start | bytes 49156
  305.1 27.9 %copy-start.1 = (bf16[2048,512]{1,0:T(8,128)(2,1)S(1)}, bf16[2048,512]{1,0:T(8,128)(2,1)}, u32[]{:S(2)}) copy-start(bf16[2048,512]{1,0:T(8,128)(2,1)} %all-gather.6.cloned.1.call-done) | copy-start | bytes 6291460
  333.0 0.9 copy-start.6
  334.5 5.1 %copy-start.9 = (u32[256]{0:T(256)S(1)}, u32[256]{0:T(256)}, u32[]{:S(2)}) copy-start(u32[256]{0:T(256)} %constant.13) | copy-start | bytes 3076
  334.5 6.4 %copy-start.4 = (bf16[128,16,320]{0,2,1:T(8,128)(2,1)S(1)}, bf16[128,16,320]{0,2,1:T(8,128)(2,1)}, u32[]{:S(2)}) copy-start(bf16[128,16,320]{0,2,1:T(8,128)(2,1)} %copy-done.3) | copy-start | bytes 3932164
  335.9 167.2 %all-to-all-start = ((bf16[16,128,320]{1,2,0:T(8,128)(2,1)}), bf16[16,128,320]{1,2,0:T(8,128)(2,1)S(1)}, u32[]{:S(2)}, u32[]{:S(2)}) async-start(bf16[16,128,320]{1,2,0:T(8,128)(2,1)} %bitcast.38), calls=%async_computation.1 | async-start | bytes 2621440 | tf_op jit(solution)/shard_map/all_to_all | solution.py:46
Sparse Core Ops, SparseCore 0:
  10.7 57.6 all-gather.3
  79.1 68.5 reduce-scatter.5
  150.7 76.1 all-gather.5
  229.1 66.0 all-gather.7
  299.1 82.4 reduce-scatter.9
  386.2 77.3 reduce-scatter.7
where the time goes:
time: 512 us; the launch traced here: 511 us
  waiting for transfers between devices  243 us (47%)
  blocking collectives  213 us (42%)
  matrix products  24.7 us (5%)
  between operations  14.9 us (3%)
  local copies, waits for them, and re-layouts  8.47 us (2%)
    psum x1, blocking collectives, shards(): grad_gain = lax.psum(gain_part, ('dp', 'tensor'))  81.5 us
    unnamed x1, blocking collectives  78.1 us
    reduce_scatter x1, waiting for transfers between devices, shards(): lax.psum_scatter(contract(token_rows, up_full, 1, 1), 'tensor', scatter_d...  67.7 us
    all_gather x1, waiting for transfers between devices, shards(): lax.all_gather(normed, 'tensor', axis=0, tiled=True)  64.6 us
    all_gather x1, waiting for transfers between devices, shards(): up_full = lax.all_gather(w_up, 'dp', axis=0, tiled=True)  60.5 us
    all_gather x1, waiting for transfers between devices, shards(): lax.all_gather(grad_pre, 'tensor', axis=0, tiled=True)  49.4 us
    all_gather x1, blocking collectives, shards(): lax.all_gather(grad_rope, 'tensor', axis=0, tiled=True)  27.9 us
    all_to_all x1, blocking collectives, shards(): lax.all_to_all(inputs, 'tensor', split_axis=1, concat_axis=0, tiled=True)  25.4 us
  transfers between devices with their start and end apart: 7, of which 4 were waited for; matrix products, arithmetic and copies ran while one was open for 4% of the time, Pallas kernels for 0%

commit v1 on v0

v1 whole, which is shorter than its diff:
```python
import jax
import jax.numpy as jnp
from jax import lax
from jax.experimental import pallas as pl
from jax.experimental.pallas import tpu as pltpu
from jax.sharding import PartitionSpec as P

MESH = pl.DeviceIdType.MESH
epsilon = 1e-06
f32 = jnp.float32
bf16 = jnp.bfloat16

SENDS = 200
RECVS = 200


def nt(a, b):
    return lax.dot_general(a, b, (((1,), (1,)), ((), ())), preferred_element_type=f32)


def nn(a, b):
    return lax.dot_general(a, b, (((1,), (0,)), ((), ())), preferred_element_type=f32)


class Place:
    def __init__(self):
        dp = lax.axis_index("dp")
        t = lax.axis_index("tensor")
        self.x = dp // 4
        self.yh = (dp // 2) % 2
        self.c = dp % 2
        self.yl = t // 8
        self.z = t % 8
        self.dp = dp
        self.t = t

    def dev(self, x=None, yh=None, c=None, yl=None, z=None):
        x = self.x if x is None else x
        yh = self.yh if yh is None else yh
        c = self.c if c is None else c
        yl = self.yl if yl is None else yl
        z = self.z if z is None else z
        return (x * 4 + yh * 2 + c, yl * 8 + z)

    def at_x(self, o):
        return (self.x + o) % 4

    def at_z(self, o):
        return (self.z + o + 8) % 8

    def at_y(self, o):
        y = (self.yh * 2 + self.yl + o) % 4
        return y // 2, y % 2

    def dev_x(self, o):
        return self.dev(x=self.at_x(o))

    def dev_z(self, o):
        return self.dev(z=self.at_z(o))

    def dev_y(self, o):
        yh, yl = self.at_y(o)
        return self.dev(yh=yh, yl=yl)


class Mail:
    def __init__(self, send_sem, recv_sem):
        self.send_sem = send_sem
        self.recv_sem = recv_sem
        self.sent = 0
        self.slots = 0
        self.open = []

    def slot(self, n=1):
        at = self.slots
        self.slots += n
        assert self.slots <= RECVS
        return at

    def send(self, src, dst, slot, device):
        at = self.sent
        self.sent += 1
        assert self.sent <= SENDS
        copy = pltpu.make_async_remote_copy(
            src_ref=src,
            dst_ref=dst,
            send_sem=self.send_sem.at[at],
            recv_sem=self.recv_sem.at[slot],
            device_id=device,
            device_id_type=MESH,
        )
        copy.start()
        self.open.append(copy)

    def wait(self, dst, slot, device):
        pltpu.make_async_remote_copy(
            src_ref=dst,
            dst_ref=dst,
            send_sem=self.send_sem.at[0],
            recv_sem=self.recv_sem.at[slot],
            device_id=device,
            device_id_type=MESH,
        ).wait_recv()

    def finish(self):
        for copy in self.open:
            copy.wait_send()


class Gather:
    def __init__(self, place, mail, block):
        self.p, self.m, self.block = place, mail, block
        self.plus = [mail.slot() for _ in range(4)]
        self.minus = [mail.slot() for _ in range(4)]

    def arrive(self, s):
        p, m = self.p, self.m
        part = (None, None) if s < 4 else (0, 1)
        m.wait(self.block(p.at_z(-s), part[0]), self.plus[s - 1], p.dev_z(1))
        m.wait(self.block(p.at_z(s), part[1]), self.minus[s - 1], p.dev_z(-1))

    def forward(self, s):
        p, m = self.p, self.m
        part = (None, None) if s < 3 else (0, 1)
        low, high = self.block(p.at_z(-s), part[0]), self.block(p.at_z(s), part[1])
        m.send(low, low, self.plus[s], p.dev_z(1))
        m.send(high, high, self.minus[s], p.dev_z(-1))


class Scatter:
    def __init__(self, place, mail, part, rows, out, plus, minus):
        self.p, self.m, self.part, self.rows = place, mail, part, rows
        self.out, self.rp, self.rm = out, plus, minus
        self.plus = [mail.slot() for _ in range(4)]
        self.minus = [mail.slot() for _ in range(4)]

    def step(self, s):
        p, m, rows = self.p, self.m, self.rows
        half = rows // 2
        if s == 0:
            self.out[0] = self.part(0, 0, rows).astype(bf16)
            m.send(self.out.at[0, pl.ds(0, half)], self.rp.at[0, pl.ds(0, half)], self.plus[0], p.dev_z(1))
            m.send(self.out.at[0, pl.ds(half, half)], self.rm.at[0, pl.ds(half, half)], self.minus[0], p.dev_z(-1))
            return
        for way, got, slots, k in ((1, self.rp, self.plus, 2 * s - 1), (-1, self.rm, self.minus, 2 * s)):
            if s == 1:
                lo = 0 if way == 1 else half
                other = half - lo
                m.wait(got.at[0, pl.ds(lo, half)], slots[0], p.dev_z(way))
                self.out[k, lo : lo + half] = (
                    self.part(k, lo, lo + half) + got[0, lo : lo + half].astype(f32)
                ).astype(bf16)
                self.out[k, other : other + half] = self.part(k, other, other + half).astype(bf16)
            else:
                m.wait(got.at[s - 1], slots[s - 1], p.dev_z(way))
                self.out[k] = (self.part(k, 0, rows) + got[s - 1].astype(f32)).astype(bf16)
            m.send(self.out.at[k], got.at[s], slots[s], p.dev_z(way))

    def last(self):
        p, m = self.p, self.m
        m.wait(self.rp.at[3], self.plus[3], p.dev_z(1))
        m.wait(self.rm.at[3], self.minus[3], p.dev_z(-1))
        return self.part(7, 0, self.rows) + self.rp[3].astype(f32) + self.rm[3].astype(f32)


def kernel(
    inputs, latent, gain, w_latent, w_rope, w_up, kv_hbm, grad_rope,
    gx, gup, glat, grope, ggain,
    kv, up, nrm, part, ga_out, ga_p, ga_m, gy_out, gy_in, gb_out, gb_p, gb_m, gay_out, gay_in,
    wx, wc, intr, ins, pre, pres, gxs,
    gw, r1, r2, a1, a2, s3, s3p, s3m, a3x, r3x, ry, rx, a12, r12, a3y, r3y, fin, rfin,
    gus, gusi, gu, gui, guy, guyi, guz, gn, rgz, rgy, rgx, rgc, gns,
    kv_sem, send_sem, recv_sem,
):
    p = Place()
    m = Mail(send_sem, recv_sem)
    x, yh, c, yl, z = p.x, p.yh, p.c, p.yl, p.z
    sib = p.dev(c=1 - c)
    ylo = p.dev(yl=1 - yl)
    ylo_other = p.dev(yl=1 - yl, c=1 - c)
    yhi = p.dev(yh=1 - yh)
    yhi_other = p.dev(yh=1 - yh, c=1 - c)

    load_kv = pltpu.make_async_copy(kv_hbm, kv, kv_sem.at[0])
    load_kv.start()

    friends = [sib, ylo_other, yhi_other]
    friends += [p.dev_y(o) for o in (1, 2, 3)] + [p.dev_x(o) for o in (1, 2, 3)]
    friends += [p.dev_z(o) for o in range(1, 8)]
    barrier = pltpu.get_barrier_semaphore()
    for friend in friends:
        pl.semaphore_signal(barrier, inc=1, device_id=friend, device_id_type=MESH)
    pl.semaphore_wait(barrier, len(friends))

    ux = [m.slot() for _ in range(6)]
    uyh = m.slot()
    usib = [m.slot() for _ in range(8)]

    def ublock(xx, hh, cc):
        return up.at[xx * 4 + hh * 2 + cc]

    mine = ublock(x, yh, c)
    m.send(w_up, mine, uyh, yhi)
    for o in (1, 3, 2):
        m.send(w_up, mine, ux[o - 1], p.dev_x(o))
    m.send(w_up, mine, usib[0], sib)
    up[p.dp] = w_up[...]

    lat = latent[...].astype(f32)
    inverse = lax.rsqrt(jnp.mean(lat * lat, axis=-1, keepdims=True) + epsilon)
    normed = lat * inverse * gain[...]
    nrm[yl, z] = normed.T.astype(bf16)

    def nblock_a(zz, half):
        if half is None:
            return nrm.at[:, zz, pl.ds(0, 256)]
        return nrm.at[half, zz, pl.ds(0, 256)]

    def nblock_b(zz, half):
        if half is None:
            return nrm.at[yl, zz, pl.ds(256, 256)]
        return nrm.at[yl, zz, pl.ds(256 + 128 * half, 128)]

    na = Gather(p, m, nblock_a)
    nb = Gather(p, m, nblock_b)
    nay = m.slot()
    nby = [m.slot() for _ in range(8)]

    def nb_over(zz, slot):
        block = nrm.at[yl, zz, pl.ds(256, 256)]
        m.send(block, block, nby[slot], ylo)

    def nb_arrive(zz, slot):
        m.wait(nrm.at[1 - yl, zz, pl.ds(256, 256)], nby[slot], ylo)

    first = nrm.at[yl, z, pl.ds(0, 256)]
    m.send(first, first, nay, ylo)
    nb.forward(0)
    nb_over(z, 0)

    wx[:, 0:512] = w_latent[...]
    wx[:, 512:576] = w_rope[...]
    wx[:, 576:640] = jnp.zeros((320, 64), bf16)
    quarter = pl.ds(pl.multiple_of(80 * x, 16), 80)
    wy = m.slot()

    def wblock(zz, half):
        if half is None:
            return wc.at[zz, quarter]
        return wc.at[zz, pl.ds(pl.multiple_of(80 * x + 48 * half, 16), 48 - 16 * half)]

    wg = Gather(p, m, wblock)
    local = pltpu.make_async_copy(wx.at[quarter], wblock(z, None), kv_sem.at[1])

    @pl.when(c == yl)
    def _():
        local.start()
        local.wait()

    across = pltpu.make_async_remote_copy(
        src_ref=wx.at[quarter],
        dst_ref=wblock(z, None),
        send_sem=send_sem.at[SENDS],
        recv_sem=recv_sem.at[wy],
        device_id=ylo_other,
        device_id_type=MESH,
    )

    @pl.when(c != yl)
    def _():
        across.start()

    def turn(i, carry):
        piece = inputs[:, pl.ds(pl.multiple_of(i * 640, 128), 640)].T
        for j in range(2):
            for h in range(2):
                lo = j * 320 + h * 160
                intr[h, 2 * i + j] = piece[lo : lo + 160]
        return carry

    m.wait(nrm.at[1 - yl, z, pl.ds(0, 256)], nay, ylo)
    na.forward(0)
    m.wait(ublock(x, 1 - yh, c), uyh, yhi)
    theirs = ublock(x, 1 - yh, c)
    for o in (1, 3, 2):
        m.send(theirs, theirs, ux[2 + o], p.dev_x(o))
    m.send(theirs, theirs, usib[1], sib)

    lax.fori_loop(0, 8, turn, 0)
    ins_slot = m.slot()
    m.send(intr.at[1 - c], ins, ins_slot, sib)
    pre[:, 512:576] = grad_rope[...]
    pre[:, 576:640] = jnp.zeros((128, 64), bf16)

    @pl.when(c != yl)
    def _():
        across.wait_send()
        across.wait_recv()

    nb.arrive(1)
    nb.forward(1)
    nb_over(p.at_z(-1), 1)
    nb_over(p.at_z(1), 2)
    na.arrive(1)
    na.forward(1)
    wg.forward(0)
    for i, o in enumerate((1, 3, 2)):
        theirs = ublock(p.at_x(-o), yh, c)
        m.wait(theirs, ux[o - 1], p.dev_x(o))
        m.send(theirs, theirs, usib[2 + i], sib)
    nb.arrive(2)
    nb.forward(2)
    nb_over(p.at_z(-2), 3)
    nb_over(p.at_z(2), 4)
    na.arrive(2)
    na.forward(2)
    wg.arrive(1)
    wg.forward(1)
    for i, o in enumerate((1, 3, 2)):
        theirs = ublock(p.at_x(-o), 1 - yh, c)
        m.wait(theirs, ux[2 + o], p.dev_x(o))
        m.send(theirs, theirs, usib[5 + i], sib)
    load_kv.wait()
    m.wait(ublock(x, yh, 1 - c), usib[0], sib)
    m.wait(ublock(x, 1 - yh, 1 - c), usib[1], sib)
    for i, o in enumerate((1, 3, 2)):
        m.wait(ublock(p.at_x(-o), yh, 1 - c), usib[2 + i], sib)
        m.wait(ublock(p.at_x(-o), 1 - yh, 1 - c), usib[5 + i], sib)

    def compute(k):
        away = 4 - (k + 1) // 2
        zd = (z + 8 + (2 * (k % 2) - 1) * away) % 8
        rows = kv[:, zd].reshape(256, 2048)
        got = nt(rows, up[...].reshape(512, 2048))
        part[k] = got.reshape(2, 128, 512)
        gy_out[k] = part[k, 1 - yl, :, 256:512].astype(bf16)

    ay = Scatter(p, m, lambda k, lo, hi: part[k, :, :, 0:256].reshape(256, 256)[lo:hi], 256, ga_out, ga_p, ga_m)

    def part_b(k, lo, hi):
        return part[k, yl, lo:hi, 256:512] + gy_in[k, lo:hi].astype(f32)

    by = Scatter(p, m, part_b, 128, gb_out, gb_p, gb_m)
    gys = [m.slot() for _ in range(8)]

    def over(k):
        m.send(gy_out.at[k], gy_in.at[k], gys[k], ylo)

    def over_in(k):
        m.wait(gy_in.at[k], gys[k], ylo)

    compute(0)
    ay.step(0)
    over(0)

    def more(k, carry):
        compute(k)
        return carry

    lax.fori_loop(1, 3, more, 0)
    over(1)
    over(2)
    over_in(0)
    by.step(0)
    lax.fori_loop(3, 8, more, 0)
    for k in range(3, 8):
        over(k)
    nb.arrive(3)
    nb.forward(3)
    nb_over(p.at_z(-3), 5)
    nb_over(p.at_z(3), 6)
    na.arrive(3)
    na.forward(3)
    ay.step(1)
    over_in(1)
    over_in(2)
    by.step(1)
    nb.arrive(4)
    nb_over(p.at_z(4), 7)
    na.arrive(4)
    wg.arrive(2)
    wg.forward(2)
    ay.step(2)
    over_in(3)
    over_in(4)
    by.step(2)
    for i, zz in enumerate((z, p.at_z(-1), p.at_z(1), p.at_z(-2), p.at_z(2), p.at_z(-3), p.at_z(3), p.at_z(4))):
        nb_arrive(zz, i)

    def up_tile(j):
        left = jnp.concatenate([nrm[i // 8, i % 8] for i in range(16)], axis=1)
        right = kv[:, :, :, pl.ds(pl.multiple_of(j * 256, 128), 256)].reshape(2048, 256)
        return nn(left, right)

    def theirs_tile(i, carry):
        gus[i] = up_tile(4 * (1 - c) + i).astype(bf16)
        return carry

    lax.fori_loop(0, 4, theirs_tile, 0)
    gus_slot = m.slot()
    m.send(gus, gusi, gus_slot, sib)
    wg.arrive(3)
    wg.forward(3)
    ay.step(3)
    over_in(5)
    over_in(6)
    by.step(3)
    m.wait(gusi, gus_slot, sib)

    def mine_tile(i, carry):
        gu[:, i] = (up_tile(4 * c + i) + gusi[i].astype(f32)).astype(bf16).reshape(4, 128, 256)
        return carry

    lax.fori_loop(0, 4, mine_tile, 0)
    gux = [m.slot() for _ in range(3)]
    for o in (1, 3, 2):
        m.send(gu.at[p.at_x(o)], gui.at[o - 1], gux[o - 1], p.dev_x(o))

    over_in(7)
    half_b = by.last()
    half_a = ay.last().reshape(2, 128, 256)
    gay_out[...] = half_a.astype(bf16)
    gay_slot = m.slot()
    m.send(gay_out.at[1 - yl], gay_in, gay_slot, ylo)

    wg.arrive(4)
    wxs = [m.slot() for _ in range(4)]

    def wquarter(xx, lo, n):
        return wc.at[pl.ds(lo, n), pl.ds(pl.multiple_of(80 * xx, 16), 80)]

    m.send(wquarter(x, 0, 8), wquarter(x, 0, 8), wxs[0], p.dev_x(1))
    m.send(wquarter(x, 0, 8), wquarter(x, 0, 8), wxs[1], p.dev_x(-1 + 4))

    m.wait(gay_in, gay_slot, ylo)
    part[0, 0, :, 0:256] = half_a[0]
    part[0, 1, :, 0:256] = half_a[1]
    own_a = part[0, yl, :, 0:256] + gay_in[...].astype(f32)
    grad_norm = jnp.concatenate([own_a, half_b], axis=1)
    lat = latent[...].astype(f32)
    inverse = lax.rsqrt(jnp.mean(lat * lat, axis=-1, keepdims=True) + epsilon)
    scaled = grad_norm * gain[...]
    inner = jnp.mean(scaled * lat, axis=-1, keepdims=True)
    pre[:, 0:512] = (inverse * scaled - lat * (inverse * inverse * inverse) * inner).astype(bf16)
    pre_slot = m.slot()
    m.send(pre, pres, pre_slot, sib)
    gsum = jnp.sum(grad_norm * lat * inverse, axis=0, keepdims=True)
    gn[...] = jnp.zeros((8, 128), f32)
    for q in range(4):
        gn[q : q + 1, :] = gsum[:, 128 * q : 128 * q + 128]
    rgz_slots = [m.slot() for _ in range(7)]
    for o in range(1, 8):
        m.send(gn, rgz.at[o - 1], rgz_slots[o - 1], p.dev_z(o))

    m.wait(ins, ins_slot, sib)
    m.wait(pres, pre_slot, sib)
    both = jnp.concatenate([pre[...], pres[...]], axis=0)

    def gw_tile(i, carry):
        at = pl.ds(4 * i, 4)
        left = jnp.concatenate(
            [intr[c, at].reshape(640, 128), ins[at].reshape(640, 128)], axis=1
        )
        got = nn(left, both[:, 0:512]).astype(bf16)
        for q in range(4):
            gw[q, at] = got[:, 128 * q : 128 * q + 128].reshape(4, 160, 128)
        return carry

    lax.fori_loop(0, 4, gw_tile, 0)
    r1_slots = [m.slot() for _ in range(3)]
    r2_slots = [m.slot() for _ in range(3)]
    for o in (2, 1, 3):
        m.send(gw.at[p.at_x(o), :, pl.ds(0, 64)], r1.at[o - 1], r1_slots[o - 1], p.dev_x(o))
        hh, ll = p.at_y(o)
        m.send(
            gw.at[:, pl.ds(8 * ll, 8), pl.ds(pl.multiple_of(64 + 32 * hh, 16), 32)],
            r2.at[o - 1], r2_slots[o - 1], p.dev_y(o),
        )

    zero = jnp.zeros((256, 64), bf16)
    rope = both[:, 512:576]
    rope_lo = jnp.concatenate([rope, zero], axis=1)
    rope_hi = jnp.concatenate([zero, rope], axis=1)

    def z3(k):
        away = 4 - (k + 1) // 2
        sign = 1 if k % 2 else -1
        return (z + 8 + sign * away) % 8

    def part3(k, lo, hi):
        zd = z3(k)
        low = jnp.concatenate([intr[c, zd], ins[zd]], axis=1)
        high = jnp.concatenate([intr[c, 8 + zd], ins[8 + zd]], axis=1)
        turned = nn(low, rope_lo) + nn(high, rope_hi)
        pieces = []
        for q in range(4):
            for ll in range(2):
                pieces.append(gw[q, 8 * ll + zd, 128:160, :].astype(f32))
        return jnp.concatenate(pieces + [turned], axis=0)[lo:hi]

    zs = Scatter(p, m, part3, 416, s3, s3p, s3m)
    for s in range(4):
        zs.step(s)
    sum3 = zs.last()
    for q in range(4):
        a3x[q, 0:64] = sum3[64 * q : 64 * q + 64].astype(bf16)
        a3x[q, 64:224] = sum3[256:416].astype(bf16)
    r3x_slots = [m.slot() for _ in range(3)]
    for o in (2, 1, 3):
        m.send(a3x.at[p.at_x(o)], r3x.at[o - 1], r3x_slots[o - 1], p.dev_x(o))

    for o in range(1, 8):
        m.wait(rgz.at[o - 1], rgz_slots[o - 1], p.dev_z(o))
    gns[0] = gn[...] + jnp.sum(rgz[...], axis=0)
    rgy_slots = [m.slot() for _ in range(3)]
    for o in (1, 2, 3):
        m.send(gns.at[0], rgy.at[o - 1], rgy_slots[o - 1], p.dev_y(o))

    for o in (1, 3, 2):
        m.wait(r1.at[o - 1], r1_slots[o - 1], p.dev_x(o))
    for h in range(2):
        rows = pl.ds(32 * h, 32)
        sum1 = gw[x, :, rows].astype(f32)
        for o in range(3):
            sum1 = sum1 + r1[o, :, rows].astype(f32)
        a1[h] = sum1.astype(bf16)
    ry_slots = [m.slot() for _ in range(3)]
    for o in (2, 1, 3):
        hh, ll = p.at_y(o)
        m.send(a1.at[hh, pl.ds(8 * ll, 8)], ry.at[o - 1], ry_slots[o - 1], p.dev_y(o))
    for o in (1, 3, 2):
        m.wait(r2.at[o - 1], r2_slots[o - 1], p.dev_y(o))
    for q in range(4):
        sum2 = gw[q, pl.ds(8 * yl, 8), pl.ds(pl.multiple_of(64 + 32 * yh, 16), 32)].astype(f32)
        for o in range(3):
            sum2 = sum2 + r2[o, q].astype(f32)
        a2[q] = sum2.astype(bf16)
    rx_slots = [m.slot() for _ in range(3)]
    for o in (2, 1, 3):
        m.send(a2.at[p.at_x(o)], rx.at[o - 1], rx_slots[o - 1], p.dev_x(o))

    for o in (1, 2, 3):
        m.wait(rgy.at[o - 1], rgy_slots[o - 1], p.dev_y(o))
    gns[1] = gns[0] + rgy[0] + rgy[1] + rgy[2]
    rgx_slots = [m.slot() for _ in range(3)]
    for o in (1, 2, 3):
        m.send(gns.at[1], rgx.at[o - 1], rgx_slots[o - 1], p.dev_x(o))

    for o in (1, 3, 2):
        m.wait(r3x.at[o - 1], r3x_slots[o - 1], p.dev_x(o))
    sum3 = a3x[x].astype(f32) + r3x[0].astype(f32) + r3x[1].astype(f32) + r3x[2].astype(f32)
    for ll in range(2):
        for hh in range(2):
            lo = 32 * ll + 16 * hh
            a3y[2 * hh + ll, 0:16] = sum3[lo : lo + 16].astype(bf16)
            a3y[2 * hh + ll, 16:176] = sum3[64:224].astype(bf16)
    r3y_slots = [m.slot() for _ in range(3)]
    for o in (2, 1, 3):
        hh, ll = p.at_y(o)
        m.send(a3y.at[2 * hh + ll], r3y.at[o - 1], r3y_slots[o - 1], p.dev_y(o))

    for o in (1, 3, 2):
        m.wait(ry.at[o - 1], ry_slots[o - 1], p.dev_y(o))
    sum1 = a1[yh, pl.ds(8 * yl, 8)].astype(f32)
    for o in range(3):
        sum1 = sum1 + ry[o].astype(f32)
    a12[:, 0:32] = sum1.astype(bf16)
    for o in (1, 3, 2):
        m.wait(rx.at[o - 1], rx_slots[o - 1], p.dev_x(o))
    sum2 = a2[x].astype(f32)
    for o in range(3):
        sum2 = sum2 + rx[o].astype(f32)
    a12[:, 32:64] = sum2.astype(bf16)
    r12_slots = [m.slot() for _ in range(7)]
    for o in range(1, 8):
        m.send(a12.at[p.at_z(o)], r12.at[o - 1], r12_slots[o - 1], p.dev_z(o))

    for o in (1, 3, 2):
        m.wait(gui.at[o - 1], gux[o - 1], p.dev_x(o))
    for h in range(2):
        rows = pl.ds(64 * h, 64)
        total = gu[x, :, rows].astype(f32)
        for o in range(3):
            total = total + gui[o, :, rows].astype(f32)
        guy[h] = total.astype(bf16)
    guy_slot = m.slot()
    m.send(guy.at[1 - yh], guyi, guy_slot, yhi)

    m.wait(wquarter(p.at_x(3), 0, 8), wxs[0], p.dev_x(1))
    m.wait(wquarter(p.at_x(1), 0, 8), wxs[1], p.dev_x(3))
    m.send(wquarter(p.at_x(3), 0, 4), wquarter(p.at_x(3), 0, 4), wxs[2], p.dev_x(1))
    m.send(wquarter(p.at_x(1), 4, 4), wquarter(p.at_x(1), 4, 4), wxs[3], p.dev_x(3))

    m.wait(guyi, guy_slot, yhi)
    total = guy[yh].astype(f32) + guyi[...].astype(f32)
    for h in range(2):
        guz[h] = total[:, 32 * h : 32 * h + 32].astype(bf16)
    guz_slot = m.slot()
    m.send(guz.at[1 - c], gup.at[c], guz_slot, sib)
    gup[c] = guz[c]

    for o in (1, 2, 3):
        m.wait(rgx.at[o - 1], rgx_slots[o - 1], p.dev_x(o))
    gns[2] = gns[1] + rgx[0] + rgx[1] + rgx[2]
    rgc_slot = m.slot()
    m.send(gns.at[2], rgc, rgc_slot, sib)

    for o in (1, 2, 3):
        m.wait(r3y.at[o - 1], r3y_slots[o - 1], p.dev_y(o))
    sum3 = a3y[2 * yh + yl].astype(f32) + r3y[0].astype(f32) + r3y[1].astype(f32) + r3y[2].astype(f32)
    fin[64:80] = sum3[0:16].astype(bf16)
    rfin[...] = sum3[16:176].astype(bf16)
    rfin_slot = m.slot()
    m.send(rfin, grope.at[c], rfin_slot, sib)
    grope[c] = rfin[...]
    for o in range(1, 8):
        m.wait(r12.at[o - 1], r12_slots[o - 1], p.dev_z(o))
    fin[0:64] = (a12[z].astype(f32) + jnp.sum(r12[...].astype(f32), axis=0)).astype(bf16)
    fin_slots = [m.slot() for _ in range(3)]
    for slot, friend in zip(fin_slots, (sib, yhi, yhi_other)):
        m.send(fin, glat.at[c, yh], slot, friend)
    glat[c, yh] = fin[...]

    m.wait(wquarter(p.at_x(2), 0, 4), wxs[2], p.dev_x(1))
    m.wait(wquarter(p.at_x(2), 4, 4), wxs[3], p.dev_x(3))

    def gx_tile(i, carry):
        got = nt(both, wc[pl.ds(2 * i, 2)].reshape(640, 640)).astype(bf16)
        at = pl.ds(pl.multiple_of(i * 640, 128), 640)
        gx[c, :, at] = got[0:128]
        gxs[:, at] = got[128:256]
        return carry

    lax.fori_loop(0, 4, gx_tile, 0)
    gx_slot = m.slot()
    m.send(gxs, gx.at[c], gx_slot, sib)

    m.wait(rgc, rgc_slot, sib)
    ggain[...] = gns[2] + rgc[...]
    m.wait(gup.at[1 - c], guz_slot, sib)
    m.wait(grope.at[1 - c], rfin_slot, sib)
    m.wait(glat.at[1 - c, yh], fin_slots[0], sib)
    m.wait(glat.at[c, 1 - yh], fin_slots[1], yhi)
    m.wait(glat.at[1 - c, 1 - yh], fin_slots[2], yhi_other)
    m.wait(gx.at[1 - c], gx_slot, sib)
    m.finish()


def shards(inputs, latent, gain, w_latent, w_rope, w_up, grad_kv, grad_rope):
    V = lambda *shape: pltpu.VMEM(shape, bf16)
    F = lambda *shape: pltpu.VMEM(shape, f32)
    whole = pl.BlockSpec(memory_space=pltpu.VMEM)
    scratch = dict(
        kv=V(2, 8, 128, 2048), up=V(16, 32, 2048), nrm=V(2, 8, 512, 128), part=F(8, 2, 128, 512),
        ga_out=V(8, 256, 256), ga_p=V(4, 256, 256), ga_m=V(4, 256, 256),
        gy_out=V(8, 128, 256), gy_in=V(8, 128, 256),
        gb_out=V(8, 128, 256), gb_p=V(4, 128, 256), gb_m=V(4, 128, 256),
        gay_out=V(2, 128, 256), gay_in=V(128, 256),
        wx=V(320, 640), wc=V(8, 320, 640), intr=V(2, 16, 160, 128), ins=V(16, 160, 128),
        pre=V(128, 640), pres=V(128, 640), gxs=V(128, 2560),
        gw=V(4, 16, 160, 128), r1=V(3, 16, 64, 128), r2=V(3, 4, 8, 32, 128),
        a1=V(2, 16, 32, 128), a2=V(4, 8, 32, 128),
        s3=V(8, 416, 128), s3p=V(4, 416, 128), s3m=V(4, 416, 128),
        a3x=V(4, 224, 128), r3x=V(3, 224, 128), ry=V(3, 8, 32, 128), rx=V(3, 8, 32, 128),
        a12=V(8, 64, 128), r12=V(7, 64, 128), a3y=V(4, 176, 128), r3y=V(3, 176, 128),
        fin=V(80, 128), rfin=V(160, 128),
        gus=V(4, 512, 256), gusi=V(4, 512, 256), gu=V(4, 4, 128, 256), gui=V(3, 4, 128, 256),
        guy=V(2, 4, 64, 256), guyi=V(4, 64, 256), guz=V(2, 4, 32, 256),
        gn=F(8, 128), rgz=F(7, 8, 128), rgy=F(3, 8, 128), rgx=F(3, 8, 128), rgc=F(8, 128), gns=F(3, 8, 128),
        kv_sem=pltpu.SemaphoreType.DMA((2,)),
        send_sem=pltpu.SemaphoreType.DMA((SENDS + 1,)),
        recv_sem=pltpu.SemaphoreType.DMA((RECVS,)),
    )

    def body(*refs):
        own = refs[:13]
        kernel(*own, **dict(zip(scratch, refs[13:])))

    gx, gup, glat, grope, ggain = pl.pallas_call(
        body,
        out_shape=(
            jax.ShapeDtypeStruct((2, 128, 2560), bf16),
            jax.ShapeDtypeStruct((2, 4, 32, 256), bf16),
            jax.ShapeDtypeStruct((2, 2, 80, 128), bf16),
            jax.ShapeDtypeStruct((2, 160, 128), bf16),
            jax.ShapeDtypeStruct((8, 128), f32),
        ),
        in_specs=[whole] * 6 + [pl.BlockSpec(memory_space=pl.ANY), whole],
        out_specs=(whole,) * 5,
        scratch_shapes=list(scratch.values()),
        compiler_params=pltpu.CompilerParams(
            collective_id=0, has_side_effects=True, vmem_limit_bytes=60 << 20
        ),
    )(
        inputs, latent, gain.reshape(1, 512), w_latent, w_rope, w_up,
        grad_kv.reshape(2, 8, 128, 2048), grad_rope,
    )
    dp = lax.axis_index("dp")
    t = lax.axis_index("tensor")
    grad_x = gx.transpose(1, 0, 2).reshape(128, 5120)
    grad_w_up = gup.transpose(2, 0, 1, 3).reshape(32, 2048)
    rows = jnp.concatenate(
        [
            glat[:, :, 0:32].reshape(2, 64, 128),
            glat[:, :, 32:64].reshape(2, 64, 128),
            glat[:, :, 64:80].reshape(2, 32, 128),
        ],
        axis=1,
    ).reshape(320, 128)
    grad_w_latent = lax.dynamic_slice_in_dim(rows, (dp % 4) * 32, 32, axis=1)
    grad_w_rope = lax.dynamic_slice_in_dim(grope.reshape(320, 128), (t // 8) * 64 + dp * 4, 4, axis=1)
    return grad_x, grad_w_up, grad_w_latent, grad_w_rope, ggain[0:4].reshape(512)


def solution(mesh):
    in_specs = (
        P(("dp", "tensor"), None),
        P(("dp", "tensor"), None),
        P(),
        P("tensor", None),
        P("tensor", None),
        P("dp", "tensor"),
        P("dp", "tensor"),
        P(("dp", "tensor"), None),
    )
    out_specs = (
        P(("dp", "tensor"), None),
        P("dp", "tensor"),
        P("tensor", "dp"),
        P("tensor", "dp"),
        P(),
    )
    return jax.shard_map(shards, mesh=mesh, in_specs=in_specs, out_specs=out_specs, check_vma=False)
```

time: 512 us -> 139 us (0.27)
  waiting for transfers between devices: 243 us -> 0 us
  blocking collectives: 213 us -> 0 us
  Pallas kernels: 0 us -> 127 us
  matrix products: 24.7 us -> 0 us
  between operations: 14.9 us -> 0.7 us
    all_gather x3 -> x0, waiting for transfers between devices: 174 us -> none  [the longest x1 64.6 us: shards(): lax.all_gather(normed, 'tensor', axis=0, tiled=True)]
    pallas_call x0 -> x1, Pallas kernels: none -> 127 us  [shards(): pl.pallas_call(body, out_shape=(jax.ShapeDtypeStruct((2, 128, 2560), bf16...]
    psum x1 -> x0, blocking collectives: 81.5 us -> none  [shards(): grad_gain = lax.psum(gain_part, ('dp', 'tensor'))]
    unnamed x1 -> x0, blocking collectives: 78.1 us -> none
    reduce_scatter x2 -> x0, waiting for transfers between devices: 67.7 us -> none  [the longest x1 67.7 us: shards(): lax.psum_scatter(contract(token_rows, up_full, 1, 1), 'tensor', scatter_d...]
    all_gather x1 -> x0, blocking collectives: 27.9 us -> none  [shards(): lax.all_gather(grad_rope, 'tensor', axis=0, tiled=True)]
    all_to_all x1 -> x0, blocking collectives: 25.4 us -> none  [shards(): lax.all_to_all(inputs, 'tensor', split_axis=1, concat_axis=0, tiled=True)]
    dot_general x6 -> x0, matrix products: 24.7 us -> none  [contract(): lax.dot_general(left, right, (((left_dim,), (right_dim,)), ((), ())), pre...]
  transfers between devices with their start and end apart: 7 -> 0, of which waited for: 4 -> 0; matrix products, arithmetic and copies ran while one was open for 4% -> 0% of each run, Pallas kernels for 0% -> 0%
where the time goes in v1:
time: 139 us
  Pallas kernels  127 us (91%)
  local copies, waits for them, and re-layouts  11.5 us (8%)
    pallas_call x1, Pallas kernels, shards(): pl.pallas_call(body, out_shape=(jax.ShapeDtypeStruct((2, 128, 2560), bf16...  127 us
    unnamed x9, local copies, waits for them, and re-layouts  5.8 us

profile of v1, /device:TPU:1, one launch (start us, length us, event | category | flops | bytes accessed | tf_op | source)
XLA Modules:
  0.0 138.9 jit_solution(13181849982170155858)
XLA Ops:
  0.7 1.5 %copy.17.refs_4_ = bf16[320,64]{1,0:T(8,128)(2,1)} copy(bf16[320,64]{0,1:T(8,128)(2,1)} %param.12) | data formatting | bytes 81920 | tf_op args[4]
  2.2 1.4 %copy.18.refs_7_ = bf16[128,64]{1,0:T(8,128)(2,1)} copy(bf16[128,64]{0,1:T(8,128)(2,1)} %param.15) | data formatting | bytes 32768 | tf_op args[7]
  3.6 126.6 %shard_map.119 = (bf16[2,128,2560]{2,1,0:T(8,128)(2,1)}, bf16[2,4,32,256]{3,2,1,0:T(8,128)(2,1)}, bf16[2,2,80,128]{3,2,1,0:T(8,128)(2,1)}, bf16[2,160,128]{2,1,0:T(8,128)(2,1)}, f32[8,128]{1,0:T(8,128)}) custom-call(bf16[128,5120]{1,0:T(8,128)(2,1)} %refs_0_.1, bf16[128,512]{1,0:T(8,128)(2,1)} %refs_1_.1, f32[1,512]{1,0:T(1,128)} %bitcast.21, ...), custom_call_target="tpu_custom_call" | custom-call | tf_op jit(solution)/shard_map/pallas_call | solution.py:679
  130.3 0.8 fusion
  131.0 0.7 slice.14
  131.8 0.1 constant_dynamic-slice_fusion.1
  131.9 0.7 copy.23
  132.6 1.0 constant_dynamic-slice_fusion
  133.5 0.7 copy.24
  134.2 1.8 %copy.19 = bf16[128,2,2560]{0,2,1:T(8,128)(2,1)S(1)} copy(bf16[128,2,2560]{2,0,1:T(8,128)(2,1)} %bitcast.14) | data formatting | bytes 2621440 | tf_op jit(solution)/shard_map/transpose | solution.py:700
  136.0 0.0 copy-start
  136.0 0.0 copy-start.1
  136.0 1.4 %copy.22 = bf16[128,5120]{1,0:T(8,128)(2,1)} copy(bf16[128,5120]{0,1:T(8,128)(2,1)S(1)} %bitcast.13) | data formatting | bytes 2621440
  137.5 0.0 copy-done
  137.5 0.1 copy.20
  137.6 0.7 reshape.43
  138.3 0.0 copy-done.1
  138.3 0.6 slice_bitcast_fusion
  (1 shorter events, 0.0 us)
Async XLA Ops:
  136.0 1.5 %copy-start = (bf16[2,4,32,256]{3,2,1,0:T(8,128)(2,1)S(1)}, bf16[2,4,32,256]{3,2,1,0:T(8,128)(2,1)}, u32[]{:S(2)}) copy-start(bf16[2,4,32,256]{3,2,1,0:T(8,128)(2,1)} %get-tuple-element.11) | copy-start | bytes 393220
  136.0 2.3 %copy-start.1 = (f32[8,128]{1,0:T(8,128)S(1)}, f32[8,128]{1,0:T(8,128)}, u32[]{:S(2)}) copy-start(f32[8,128]{1,0:T(8,128)} %get-tuple-element.14) | copy-start | bytes 12292

commit v2 on v1

v2 whole, which is shorter than its diff:
```python
import jax
import jax.numpy as jnp
from jax import lax
from jax.experimental import pallas as pl
from jax.experimental.pallas import tpu as pltpu
from jax.sharding import PartitionSpec as P

MESH = pl.DeviceIdType.MESH
epsilon = 1e-06
f32 = jnp.float32
bf16 = jnp.bfloat16

SENDS = 260
RECVS = 260


def nt(a, b):
    return lax.dot_general(a, b, (((1,), (1,)), ((), ())), preferred_element_type=f32)


def nn(a, b):
    return lax.dot_general(a, b, (((1,), (0,)), ((), ())), preferred_element_type=f32)


class Place:
    def __init__(self):
        dp = lax.axis_index("dp")
        t = lax.axis_index("tensor")
        self.x = dp // 4
        self.yh = (dp // 2) % 2
        self.c = dp % 2
        self.yl = t // 8
        self.z = t % 8
        self.dp = dp
        self.t = t

    def dev(self, x=None, yh=None, c=None, yl=None, z=None):
        x = self.x if x is None else x
        yh = self.yh if yh is None else yh
        c = self.c if c is None else c
        yl = self.yl if yl is None else yl
        z = self.z if z is None else z
        return (x * 4 + yh * 2 + c, yl * 8 + z)

    def at_x(self, o):
        return (self.x + o) % 4

    def at_z(self, o):
        return (self.z + o + 8) % 8

    def at_y(self, o):
        y = (self.yh * 2 + self.yl + o) % 4
        return y // 2, y % 2

    def dev_x(self, o):
        return self.dev(x=self.at_x(o))

    def dev_z(self, o):
        return self.dev(z=self.at_z(o))

    def dev_y(self, o):
        yh, yl = self.at_y(o)
        return self.dev(yh=yh, yl=yl)


class Mail:
    def __init__(self, send_sem, recv_sem):
        self.send_sem = send_sem
        self.recv_sem = recv_sem
        self.sent = 0
        self.slots = 0
        self.open = []

    def slot(self, n=1):
        at = self.slots
        self.slots += n
        assert self.slots <= RECVS
        return at

    def send(self, src, dst, slot, device):
        at = self.sent
        self.sent += 1
        assert self.sent <= SENDS
        copy = pltpu.make_async_remote_copy(
            src_ref=src,
            dst_ref=dst,
            send_sem=self.send_sem.at[at],
            recv_sem=self.recv_sem.at[slot],
            device_id=device,
            device_id_type=MESH,
        )
        copy.start()
        self.open.append(copy)

    def wait(self, dst, slot, device):
        pltpu.make_async_remote_copy(
            src_ref=dst,
            dst_ref=dst,
            send_sem=self.send_sem.at[0],
            recv_sem=self.recv_sem.at[slot],
            device_id=device,
            device_id_type=MESH,
        ).wait_recv()

    def finish(self):
        for copy in self.open:
            copy.wait_send()


class Gather:
    def __init__(self, place, mail, block):
        self.p, self.m, self.block = place, mail, block
        self.plus = [mail.slot() for _ in range(4)]
        self.minus = [mail.slot() for _ in range(4)]

    def arrive(self, s):
        p, m = self.p, self.m
        part = (None, None) if s < 4 else (0, 1)
        m.wait(self.block(p.at_z(-s), part[0]), self.plus[s - 1], p.dev_z(1))
        m.wait(self.block(p.at_z(s), part[1]), self.minus[s - 1], p.dev_z(-1))

    def forward(self, s):
        p, m = self.p, self.m
        part = (None, None) if s < 3 else (0, 1)
        low, high = self.block(p.at_z(-s), part[0]), self.block(p.at_z(s), part[1])
        m.send(low, low, self.plus[s], p.dev_z(1))
        m.send(high, high, self.minus[s], p.dev_z(-1))


class Scatter:
    def __init__(self, place, mail, part, rows, out, plus, minus):
        self.p, self.m, self.part, self.rows = place, mail, part, rows
        self.out, self.rp, self.rm = out, plus, minus
        self.plus = [mail.slot() for _ in range(4)]
        self.minus = [mail.slot() for _ in range(4)]

    def step(self, s):
        p, m, rows = self.p, self.m, self.rows
        half = rows // 2
        if s == 0:
            self.out[0] = self.part(0, 0, rows).astype(bf16)
            m.send(self.out.at[0, pl.ds(0, half)], self.rp.at[0, pl.ds(0, half)], self.plus[0], p.dev_z(1))
            m.send(self.out.at[0, pl.ds(half, half)], self.rm.at[0, pl.ds(half, half)], self.minus[0], p.dev_z(-1))
            return
        for way, got, slots, k in ((1, self.rp, self.plus, 2 * s - 1), (-1, self.rm, self.minus, 2 * s)):
            if s == 1:
                lo = 0 if way == 1 else half
                other = half - lo
                m.wait(got.at[0, pl.ds(lo, half)], slots[0], p.dev_z(way))
                self.out[k, lo : lo + half] = (
                    self.part(k, lo, lo + half) + got[0, lo : lo + half].astype(f32)
                ).astype(bf16)
                self.out[k, other : other + half] = self.part(k, other, other + half).astype(bf16)
            else:
                m.wait(got.at[s - 1], slots[s - 1], p.dev_z(way))
                self.out[k] = (self.part(k, 0, rows) + got[s - 1].astype(f32)).astype(bf16)
            m.send(self.out.at[k], got.at[s], slots[s], p.dev_z(way))

    def last(self):
        p, m = self.p, self.m
        m.wait(self.rp.at[3], self.plus[3], p.dev_z(1))
        m.wait(self.rm.at[3], self.minus[3], p.dev_z(-1))
        return self.part(7, 0, self.rows) + self.rp[3].astype(f32) + self.rm[3].astype(f32)


def kernel(
    inputs_hbm, latent, gain, w_latent, w_rope, w_up, kv_hbm, grad_rope,
    gx, gup, glat, grope, ggain,
    inputs, kv, up, nrm, part, ga_out, ga_p, ga_m, gy_out, gy_in, gb_out, gb_p, gb_m, gay_out, gay_in, gnorm,
    wx, wq, wa, wc, intr, ins, pre, pres, gxs,
    rp, rps, gw, gw3, r1, r2, r3z, a1, a2, s3, s3p, s3m, a3x, r3x, ry, rx, a12, r12, a3y, r3y, fin, rfin, glatb, gropeb, gupb,
    gus, gusi, gu, gui, guy, guyi, guz, gn, rgz, rgy, rgx, rgc, gns,
    kv_sem, send_sem, recv_sem,
):
    p = Place()
    m = Mail(send_sem, recv_sem)
    x, yh, c, yl, z = p.x, p.yh, p.c, p.yl, p.z
    sib = p.dev(c=1 - c)
    ylo = p.dev(yl=1 - yl)
    ylo_other = p.dev(yl=1 - yl, c=1 - c)
    yhi = p.dev(yh=1 - yh)
    yhi_other = p.dev(yh=1 - yh, c=1 - c)

    load_inputs = pltpu.make_async_copy(inputs_hbm, inputs, kv_sem.at[1])
    load_inputs.start()
    load_kv = pltpu.make_async_copy(kv_hbm, kv, kv_sem.at[0])
    load_kv.start()

    friends = [sib, ylo_other, yhi_other]
    friends += [p.dev_y(o) for o in (1, 2, 3)] + [p.dev_x(o) for o in (1, 2, 3)]
    friends += [p.dev_z(o) for o in range(1, 8)]
    barrier = pltpu.get_barrier_semaphore()
    for friend in friends:
        pl.semaphore_signal(barrier, inc=1, device_id=friend, device_id_type=MESH)

    lat = latent[...].astype(f32)
    inverse = lax.rsqrt(jnp.mean(lat * lat, axis=-1, keepdims=True) + epsilon)
    normed = lat * inverse * gain[...]
    nrm[yl, z] = normed.T.astype(bf16)
    up[p.dp] = w_up[...]

    y = yh * 2 + yl
    wx[:, 0:512] = w_latent[...]
    wx[:, 512:576] = w_rope[...].T
    wx[:, 576:640] = jnp.zeros((320, 64), bf16)

    def xrows(at):
        return pl.ds(pl.multiple_of(48 * at, 16), 48)

    def yrows(at):
        return pl.ds(pl.multiple_of(192 + 32 * at, 16), 32)

    wa[0:48] = wx[xrows(x)]
    wa[48:80] = wx[yrows(yh * 2 + 1 - yl)]

    @pl.when(c == yl)
    def _():
        wq[z, 0:48] = wx[xrows(x)]
        wq[z, 48:80] = wx[yrows(y)]

    pre[:, 512:576] = grad_rope[...].T
    pre[:, 576:640] = jnp.zeros((128, 64), bf16)
    rp[...] = pre[:, 512:640]

    def turn(i, carry):
        piece = inputs[:, pl.ds(pl.multiple_of(i * 640, 128), 640)].T
        for j in range(2):
            for h in range(2):
                lo = j * 320 + h * 160
                intr[h, 2 * i + j] = piece[lo : lo + 160]
        return carry

    load_inputs.wait()
    lax.fori_loop(0, 8, turn, 0)

    pl.semaphore_wait(barrier, len(friends))

    ux = [m.slot() for _ in range(6)]
    uyh = m.slot()
    usib = [m.slot() for _ in range(8)]

    def ublock(xx, hh, cc):
        return up.at[xx * 4 + hh * 2 + cc]

    mine = ublock(x, yh, c)
    m.send(mine, mine, uyh, yhi)
    for o in (3, 1, 2):
        m.send(mine, mine, ux[o - 1], p.dev_x(o))
    m.send(mine, mine, usib[0], sib)

    def nblock_a(zz, half):
        if half is None:
            return nrm.at[:, zz, pl.ds(0, 256)]
        return nrm.at[half, zz, pl.ds(0, 256)]

    def nblock_b(zz, half):
        if half is None:
            return nrm.at[yl, zz, pl.ds(256, 256)]
        return nrm.at[yl, zz, pl.ds(256 + 128 * half, 128)]

    na = Gather(p, m, nblock_a)
    nb = Gather(p, m, nblock_b)
    nay = m.slot()
    nby = [m.slot() for _ in range(8)]

    def nb_over(zz, slot):
        block = nrm.at[yl, zz, pl.ds(256, 256)]
        m.send(block, block, nby[slot], ylo)

    def nb_arrive(zz, slot):
        m.wait(nrm.at[1 - yl, zz, pl.ds(256, 256)], nby[slot], ylo)

    first = nrm.at[yl, z, pl.ds(0, 256)]
    m.send(first, first, nay, ylo)
    wy = m.slot()
    across = pltpu.make_async_remote_copy(
        src_ref=wa,
        dst_ref=wq.at[z],
        send_sem=send_sem.at[SENDS],
        recv_sem=recv_sem.at[wy],
        device_id=ylo_other,
        device_id_type=MESH,
    )

    nb.forward(0)
    ins_slot = m.slot()
    m.send(intr.at[1 - c], ins, ins_slot, sib)
    rp_slot = m.slot()
    m.send(rp, rps, rp_slot, sib)

    def wblock(zz, half):
        if half is None:
            return wq.at[zz]
        return wq.at[zz, pl.ds(48 * half, 48 - 16 * half)]

    wg = Gather(p, m, wblock)
    offsets = (0, -1, 1, -2, 2, -3, 3, 4)
    onward = {0: 1, -1: 1, -2: 1, -3: 1, 1: 3, 2: 3, 3: 3, 4: 3}
    wslots = {(o, a, d): m.slot() for o in offsets for a in "xy" for d in (1, 3, 2)}

    def wdone(o, a, at):
        zz = p.at_z(o)
        if a == "x":
            return wc.at[zz, xrows((x + at) % 4)]
        return wc.at[zz, yrows((y + at) % 4)]

    def wsend(*which):
        for o in which:
            zz = p.at_z(o)
            for d in (1, 3):
                m.send(wq.at[zz, pl.ds(0, 48)], wdone(o, "x", 0), wslots[o, "x", d], p.dev_x(d))
                m.send(wq.at[zz, pl.ds(48, 32)], wdone(o, "y", 0), wslots[o, "y", d], p.dev_y(d))

    def wonward(*which):
        for o in which:
            for a, dev in (("x", p.dev_x), ("y", p.dev_y)):
                for d in (1, 3):
                    m.wait(wdone(o, a, 4 - d), wslots[o, a, d], dev(d))
                d = onward[o]
                m.send(wdone(o, a, 4 - d), wdone(o, a, 4 - d), wslots[o, a, 2], dev(d))

    def wlast(*which):
        for o in which:
            for a, dev in (("x", p.dev_x), ("y", p.dev_y)):
                m.wait(wdone(o, a, 2), wslots[o, a, 2], dev(onward[o]))
            zz = p.at_z(o)
            wc[zz, xrows(x)] = wq[zz, 0:48]
            wc[zz, yrows(y)] = wq[zz, 48:80]

    m.wait(ublock(x, 1 - yh, c), uyh, yhi)
    theirs = ublock(x, 1 - yh, c)
    for o in (3, 1, 2):
        m.send(theirs, theirs, ux[2 + o], p.dev_x(o))
    m.send(theirs, theirs, usib[1], sib)

    @pl.when(c != yl)
    def _():
        across.start()

    m.wait(nrm.at[1 - yl, z, pl.ds(0, 256)], nay, ylo)
    na.forward(0)
    nb_over(z, 0)

    @pl.when(c != yl)
    def _():
        across.wait_send()
        across.wait_recv()

    wg.forward(0)
    nb.arrive(1)
    nb.forward(1)
    nb_over(p.at_z(-1), 1)
    nb_over(p.at_z(1), 2)
    na.arrive(1)
    na.forward(1)
    wg.arrive(1)
    wg.forward(1)

    def up_arrive(hh, base, *which):
        for o in which:
            theirs = ublock(p.at_x(-o), hh, c)
            m.wait(theirs, ux[base + o], p.dev_x(o))
            m.send(theirs, theirs, usib[2 + base + o], sib)

    def up_across(*which):
        for o in which:
            m.wait(ublock(p.at_x(-o), yh, 1 - c), usib[1 + o], sib)
            m.wait(ublock(p.at_x(-o), 1 - yh, 1 - c), usib[4 + o], sib)

    up_arrive(yh, -1, 3, 1, 2)
    nb.arrive(2)
    nb.forward(2)
    nb_over(p.at_z(-2), 3)
    nb_over(p.at_z(2), 4)
    na.arrive(2)
    na.forward(2)
    load_kv.wait()
    m.wait(ublock(x, yh, 1 - c), usib[0], sib)
    m.wait(ublock(x, 1 - yh, 1 - c), usib[1], sib)
    up_arrive(1 - yh, 2, 3)
    up_across(3)

    def away(k):
        return (z + 8 + (2 * (k % 2) - 1) * (4 - (k + 1) // 2)) % 8

    def compute(k, half):
        rows = kv[:, away(k)].reshape(256, 2048)
        heads = jnp.concatenate(
            [up[pl.ds(4 * p.at_x(2 * half + i), 4)].reshape(128, 2048) for i in range(2)], axis=0
        )
        part[k, :, :, 256 * half : 256 * half + 256] = nt(rows, heads).reshape(2, 128, 256)
        if half == 1:
            gy_out[k] = part[k, 1 - yl, :, 256:512].astype(bf16)

    def part_a(at):
        def get(k, lo, hi):
            return part[k, :, :, 128 * at : 128 * at + 128].reshape(256, 128)[lo:hi]

        return get

    a0 = Scatter(p, m, part_a(0), 256, ga_out.at[0], ga_p.at[0], ga_m.at[0])
    a1s = Scatter(p, m, part_a(1), 256, ga_out.at[1], ga_p.at[1], ga_m.at[1])

    def part_b(k, lo, hi):
        return part[k, yl, lo:hi, 256:512] + gy_in[k, lo:hi].astype(f32)

    by = Scatter(p, m, part_b, 128, gb_out, gb_p, gb_m)
    gys = [m.slot() for _ in range(8)]

    def over(k):
        m.send(gy_out.at[k], gy_in.at[k], gys[k], ylo)

    def over_in(k):
        m.wait(gy_in.at[k], gys[k], ylo)

    m.wait(ins, ins_slot, sib)
    m.wait(rps, rp_slot, sib)

    def part_r(k, lo, hi):
        away = 4 - (k + 1) // 2
        sign = 1 if k % 2 else -1
        zd = (z + 8 + sign * away) % 8
        rope = jnp.concatenate([rp[:, 0:64], rps[:, 0:64]], axis=0)
        none = jnp.zeros((256, 64), bf16)
        low = jnp.concatenate([intr[c, zd], ins[zd]], axis=1)
        high = jnp.concatenate([intr[c, 8 + zd], ins[8 + zd]], axis=1)
        turned = nn(low, jnp.concatenate([rope, none], axis=1)) + nn(high, jnp.concatenate([none, rope], axis=1))
        return turned[lo:hi]

    rs = Scatter(p, m, part_r, 160, s3, s3p, s3m)

    def up_tile(j):
        left = jnp.concatenate([nrm[i // 8, i % 8] for i in range(16)], axis=1)
        right = kv[:, :, :, pl.ds(pl.multiple_of(j * 256, 128), 256)].reshape(2048, 256)
        return nn(left, right)

    def theirs_tile(i, carry):
        gus[i] = up_tile(4 * (1 - c) + i).astype(bf16)
        return carry

    def mine_tile(i, carry):
        gu[:, i] = (up_tile(4 * c + i) + gusi[i].astype(f32)).astype(bf16).reshape(4, 128, 256)
        return carry

    def more(half):
        def body(k, carry):
            compute(k, half)
            return carry

        return body

    compute(0, 0)
    a0.step(0)
    a1s.step(0)
    lax.fori_loop(1, 3, more(0), 0)
    a0.step(1)
    a1s.step(1)
    up_arrive(1 - yh, 2, 1, 2)
    wsend(0, -1, 1)
    up_across(1, 2)
    compute(0, 1)
    over(0)
    lax.fori_loop(1, 3, more(1), 0)
    over(1)
    over(2)
    lax.fori_loop(3, 5, more(0), 0)
    a0.step(2)
    a1s.step(2)
    lax.fori_loop(3, 8, more(1), 0)
    for k in range(3, 8):
        over(k)
    over_in(0)
    by.step(0)
    lax.fori_loop(5, 8, more(0), 0)
    wg.arrive(2)
    wg.forward(2)
    wsend(-2, 2)
    nb.arrive(3)
    nb.forward(3)
    nb_over(p.at_z(-3), 5)
    nb_over(p.at_z(3), 6)
    na.arrive(3)
    na.forward(3)
    a0.step(3)
    a1s.step(3)
    over_in(1)
    over_in(2)
    by.step(1)
    wg.arrive(3)
    wg.forward(3)
    wsend(-3, 3)
    rs.step(0)
    nb.arrive(4)
    nb_over(p.at_z(4), 7)
    over_in(3)
    over_in(4)
    by.step(2)
    gay_slots = [m.slot() for _ in range(2)]
    for i, chain in enumerate((a0, a1s)):
        half_a = chain.last().reshape(2, 128, 128)
        gay_out[i] = half_a.astype(bf16)
        m.send(gay_out.at[i, 1 - yl], gay_in.at[i], gay_slots[i], ylo)
        for h in range(2):
            part[0, h, :, 128 * i : 128 * i + 128] = half_a[h]
    na.arrive(4)
    wg.arrive(4)
    wsend(4)
    rs.step(1)
    over_in(5)
    over_in(6)
    by.step(3)
    wonward(0, -1, 1)
    over_in(7)
    part[0, 0, :, 256:512] = by.last()
    for i in range(2):
        m.wait(gay_in.at[i], gay_slots[i], ylo)
    own_a = part[0, yl, :, 0:256] + jnp.concatenate([gay_in[0], gay_in[1]], axis=1).astype(f32)
    for i in range(2):
        gnorm[:, pl.ds(pl.multiple_of(128 * p.at_x(i), 128), 128)] = own_a[:, 128 * i : 128 * i + 128]
        gnorm[:, pl.ds(pl.multiple_of(128 * p.at_x(2 + i), 128), 128)] = part[0, 0, :, 256 + 128 * i : 384 + 128 * i]
    grad_norm = gnorm[...]
    lat = latent[...].astype(f32)
    inverse = lax.rsqrt(jnp.mean(lat * lat, axis=-1, keepdims=True) + epsilon)
    scaled = grad_norm * gain[...]
    inner = jnp.mean(scaled * lat, axis=-1, keepdims=True)
    pre[:, 0:512] = (inverse * scaled - lat * (inverse * inverse * inverse) * inner).astype(bf16)
    pre_slot = m.slot()
    m.send(pre, pres, pre_slot, sib)
    gsum = jnp.sum(grad_norm * lat * inverse, axis=0, keepdims=True)
    gn[...] = jnp.zeros((8, 128), f32)
    for q in range(4):
        gn[q : q + 1, :] = gsum[:, 128 * q : 128 * q + 128]
    rgz_slots = [m.slot() for _ in range(7)]
    for o in range(1, 8):
        m.send(gn, rgz.at[o - 1], rgz_slots[o - 1], p.dev_z(o))

    m.wait(pres, pre_slot, sib)
    both = jnp.concatenate([pre[...], pres[...]], axis=0)

    def gw_tile(i, carry):
        at = pl.ds(4 * i, 4)
        left = jnp.concatenate(
            [intr[c, at].reshape(640, 128), ins[at].reshape(640, 128)], axis=1
        )
        got = nn(left, both[:, 0:512]).astype(bf16)
        for q in range(4):
            piece = got[:, 128 * q : 128 * q + 128].reshape(4, 160, 128)
            gw[q, at] = piece[:, 0:128]
            for j in range(4):
                gw3[4 * (i % 2) + j, q, i // 2] = piece[j, 128:160]
        return carry

    lax.fori_loop(0, 4, gw_tile, 0)
    r3z_slots = [m.slot() for _ in range(7)]
    for o in (4, 3, 5, 2, 6, 1, 7):
        m.send(gw3.at[p.at_z(o)], r3z.at[o - 1], r3z_slots[o - 1], p.dev_z(o))
    r1_slots = [m.slot() for _ in range(3)]
    r2_slots = [m.slot() for _ in range(3)]
    for o in (2, 1, 3):
        m.send(gw.at[p.at_x(o), :, pl.ds(0, 64)], r1.at[o - 1], r1_slots[o - 1], p.dev_x(o))
        hh, ll = p.at_y(o)
        m.send(
            gw.at[:, pl.ds(8 * ll, 8), pl.ds(pl.multiple_of(64 + 32 * hh, 16), 32)],
            r2.at[o - 1], r2_slots[o - 1], p.dev_y(o),
        )

    for i, o in enumerate((0, -1, 1, -2, 2, -3, 3, 4)):
        nb_arrive(p.at_z(o), i)
    lax.fori_loop(0, 4, theirs_tile, 0)
    gus_slot = m.slot()
    m.send(gus, gusi, gus_slot, sib)
    m.wait(gusi, gus_slot, sib)
    lax.fori_loop(0, 4, mine_tile, 0)
    gux = [m.slot() for _ in range(3)]
    for o in (1, 3, 2):
        m.send(gu.at[p.at_x(o)], gui.at[o - 1], gux[o - 1], p.dev_x(o))
    rs.step(2)
    wonward(-2, 2, -3, 3, 4)
    rs.step(3)
    turned = rs.last().astype(bf16)
    for o in (1, 7, 2, 6, 3, 5, 4):
        m.wait(r3z.at[o - 1], r3z_slots[o - 1], p.dev_z(o))
    for q in range(4):
        sum3 = gw3[z, q].astype(f32)
        for o in range(7):
            sum3 = sum3 + r3z[o, q].astype(f32)
        a3x[q, 0:64] = sum3.reshape(64, 128).astype(bf16)
        a3x[q, 64:224] = turned
    r3x_slots = [m.slot() for _ in range(3)]
    for o in (2, 1, 3):
        m.send(a3x.at[p.at_x(o)], r3x.at[o - 1], r3x_slots[o - 1], p.dev_x(o))

    for o in range(1, 8):
        m.wait(rgz.at[o - 1], rgz_slots[o - 1], p.dev_z(o))
    gns[0] = gn[...] + jnp.sum(rgz[...], axis=0)
    rgy_slots = [m.slot() for _ in range(3)]
    for o in (1, 2, 3):
        m.send(gns.at[0], rgy.at[o - 1], rgy_slots[o - 1], p.dev_y(o))

    for o in (1, 3, 2):
        m.wait(r1.at[o - 1], r1_slots[o - 1], p.dev_x(o))
    for h in range(2):
        rows = pl.ds(32 * h, 32)
        sum1 = gw[x, :, rows].astype(f32)
        for o in range(3):
            sum1 = sum1 + r1[o, :, rows].astype(f32)
        a1[h] = sum1.astype(bf16)
    ry_slots = [m.slot() for _ in range(3)]
    for o in (2, 1, 3):
        hh, ll = p.at_y(o)
        m.send(a1.at[hh, pl.ds(8 * ll, 8)], ry.at[o - 1], ry_slots[o - 1], p.dev_y(o))
    for o in (1, 3, 2):
        m.wait(r2.at[o - 1], r2_slots[o - 1], p.dev_y(o))
    for q in range(4):
        sum2 = gw[q, pl.ds(8 * yl, 8), pl.ds(pl.multiple_of(64 + 32 * yh, 16), 32)].astype(f32)
        for o in range(3):
            sum2 = sum2 + r2[o, q].astype(f32)
        a2[q] = sum2.astype(bf16)
    rx_slots = [m.slot() for _ in range(3)]
    for o in (2, 1, 3):
        m.send(a2.at[p.at_x(o)], rx.at[o - 1], rx_slots[o - 1], p.dev_x(o))

    for o in (1, 2, 3):
        m.wait(rgy.at[o - 1], rgy_slots[o - 1], p.dev_y(o))
    gns[1] = gns[0] + rgy[0] + rgy[1] + rgy[2]
    rgx_slots = [m.slot() for _ in range(3)]
    for o in (1, 2, 3):
        m.send(gns.at[1], rgx.at[o - 1], rgx_slots[o - 1], p.dev_x(o))

    for o in (1, 3, 2):
        m.wait(r3x.at[o - 1], r3x_slots[o - 1], p.dev_x(o))
    sum3 = a3x[x].astype(f32) + r3x[0].astype(f32) + r3x[1].astype(f32) + r3x[2].astype(f32)
    for ll in range(2):
        for hh in range(2):
            lo = 32 * ll + 16 * hh
            a3y[2 * hh + ll, 0:16] = sum3[lo : lo + 16].astype(bf16)
            a3y[2 * hh + ll, 16:176] = sum3[64:224].astype(bf16)
    r3y_slots = [m.slot() for _ in range(3)]
    for o in (2, 1, 3):
        hh, ll = p.at_y(o)
        m.send(a3y.at[2 * hh + ll], r3y.at[o - 1], r3y_slots[o - 1], p.dev_y(o))

    wlast(0, -1, 1, -2, 2, -3, 3, 4)

    own_columns = pl.multiple_of(2560 * c, 128)

    def gx_tile(i, carry):
        got = nt(both, wc[pl.ds(2 * i, 2)].reshape(640, 640)).astype(bf16)
        gx[:, pl.ds(pl.multiple_of(own_columns + i * 640, 128), 640)] = got[0:128]
        gxs[:, pl.ds(pl.multiple_of(i * 640, 128), 640)] = got[128:256]
        return carry

    lax.fori_loop(0, 4, gx_tile, 0)
    gx_slot = m.slot()
    m.send(gxs, gx.at[:, pl.ds(own_columns, 2560)], gx_slot, sib)
    for o in (1, 3, 2):
        m.wait(ry.at[o - 1], ry_slots[o - 1], p.dev_y(o))
    sum1 = a1[yh, pl.ds(8 * yl, 8)].astype(f32)
    for o in range(3):
        sum1 = sum1 + ry[o].astype(f32)
    a12[:, 0:32] = sum1.astype(bf16)
    for o in (1, 3, 2):
        m.wait(rx.at[o - 1], rx_slots[o - 1], p.dev_x(o))
    sum2 = a2[x].astype(f32)
    for o in range(3):
        sum2 = sum2 + rx[o].astype(f32)
    a12[:, 32:64] = sum2.astype(bf16)
    r12_slots = [m.slot() for _ in range(7)]
    for o in range(1, 8):
        m.send(a12.at[p.at_z(o)], r12.at[o - 1], r12_slots[o - 1], p.dev_z(o))

    for o in (1, 3, 2):
        m.wait(gui.at[o - 1], gux[o - 1], p.dev_x(o))
    for h in range(2):
        rows = pl.ds(64 * h, 64)
        total = gu[x, :, rows].astype(f32)
        for o in range(3):
            total = total + gui[o, :, rows].astype(f32)
        guy[h] = total.astype(bf16)
    guy_slot = m.slot()
    m.send(guy.at[1 - yh], guyi, guy_slot, yhi)

    m.wait(guyi, guy_slot, yhi)
    total = guy[yh].astype(f32) + guyi[...].astype(f32)
    for h in range(2):
        guz[h] = total[:, 32 * h : 32 * h + 32].astype(bf16)
    guz_slot = m.slot()
    m.send(guz.at[1 - c], gupb, guz_slot, sib)
    for i in range(4):
        gup[:, pl.ds(pl.multiple_of(1024 * c + 256 * i, 128), 256)] = guz[c, i]

    for o in (1, 2, 3):
        m.wait(rgx.at[o - 1], rgx_slots[o - 1], p.dev_x(o))
    gns[2] = gns[1] + rgx[0] + rgx[1] + rgx[2]
    rgc_slot = m.slot()
    m.send(gns.at[2], rgc, rgc_slot, sib)

    for o in (1, 2, 3):
        m.wait(r3y.at[o - 1], r3y_slots[o - 1], p.dev_y(o))
    sum3 = a3y[2 * yh + yl].astype(f32) + r3y[0].astype(f32) + r3y[1].astype(f32) + r3y[2].astype(f32)
    fin[64:80] = sum3[0:16].astype(bf16)
    rfin[...] = sum3[16:176].astype(bf16)
    rfin_slot = m.slot()
    m.send(rfin, gropeb.at[c], rfin_slot, sib)
    gropeb[c] = rfin[...]
    for o in range(1, 8):
        m.wait(r12.at[o - 1], r12_slots[o - 1], p.dev_z(o))
    fin[0:64] = (a12[z].astype(f32) + jnp.sum(r12[...].astype(f32), axis=0)).astype(bf16)
    fin_slots = [m.slot() for _ in range(3)]
    for slot, friend in zip(fin_slots, (sib, yhi, yhi_other)):
        m.send(fin, glatb.at[c, yh], slot, friend)
    glatb[c, yh] = fin[...]

    m.wait(rgc, rgc_slot, sib)
    total = gns[2] + rgc[...]
    for q in range(4):
        ggain[:, 128 * q : 128 * q + 128] = total[q : q + 1]
    m.wait(gupb, guz_slot, sib)
    for i in range(4):
        gup[:, pl.ds(pl.multiple_of(1024 * (1 - c) + 256 * i, 128), 256)] = gupb[i]

    def columns(first, n, rows):
        row = lax.broadcasted_iota(jnp.int32, (n, 128), 0)
        column = lax.broadcasted_iota(jnp.int32, (n, 128), 1)
        return nt((column == row + first).astype(bf16), rows).astype(bf16)

    m.wait(gropeb.at[1 - c], rfin_slot, sib)
    grope[...] = columns(yl * 64 + p.dp * 4, 16, gropeb[...].reshape(320, 128))[0:4]
    m.wait(glatb.at[1 - c, yh], fin_slots[0], sib)
    m.wait(glatb.at[c, 1 - yh], fin_slots[1], yhi)
    m.wait(glatb.at[1 - c, 1 - yh], fin_slots[2], yhi_other)
    rows = []
    for h in range(2):
        for lo, n in ((0, 32), (32, 32), (64, 16)):
            for i in range(2):
                rows.append(glatb[h, i, lo : lo + n])
    glat[...] = columns((p.dp % 4) * 32, 32, jnp.concatenate(rows, axis=0))
    m.wait(gx.at[:, pl.ds(pl.multiple_of(2560 * (1 - c), 128), 2560)], gx_slot, sib)
    m.finish()


def shards(inputs, latent, gain, w_latent, w_rope, w_up, grad_kv, grad_rope):
    V = lambda *shape: pltpu.VMEM(shape, bf16)
    F = lambda *shape: pltpu.VMEM(shape, f32)
    whole = pl.BlockSpec(memory_space=pltpu.VMEM)
    scratch = dict(
        inputs=V(128, 5120), kv=V(2, 8, 128, 2048), up=V(16, 32, 2048), nrm=V(2, 8, 512, 128), part=F(8, 2, 128, 512),
        ga_out=V(2, 8, 256, 128), ga_p=V(2, 4, 256, 128), ga_m=V(2, 4, 256, 128),
        gy_out=V(8, 128, 256), gy_in=V(8, 128, 256),
        gb_out=V(8, 128, 256), gb_p=V(4, 128, 256), gb_m=V(4, 128, 256),
        gay_out=V(2, 2, 128, 128), gay_in=V(2, 128, 128), gnorm=F(128, 512),
        wx=V(320, 640), wq=V(8, 80, 640), wa=V(80, 640), wc=V(8, 320, 640), intr=V(2, 16, 160, 128), ins=V(16, 160, 128),
        pre=V(128, 640), pres=V(128, 640), gxs=V(128, 2560),
        rp=V(128, 128), rps=V(128, 128), gw=V(4, 16, 128, 128), gw3=V(8, 4, 2, 32, 128), r1=V(3, 16, 64, 128), r2=V(3, 4, 8, 32, 128), r3z=V(7, 4, 2, 32, 128),
        a1=V(2, 16, 32, 128), a2=V(4, 8, 32, 128),
        s3=V(8, 160, 128), s3p=V(4, 160, 128), s3m=V(4, 160, 128),
        a3x=V(4, 224, 128), r3x=V(3, 224, 128), ry=V(3, 8, 32, 128), rx=V(3, 8, 32, 128),
        a12=V(8, 64, 128), r12=V(7, 64, 128), a3y=V(4, 176, 128), r3y=V(3, 176, 128),
        fin=V(80, 128), rfin=V(160, 128), glatb=V(2, 2, 80, 128), gropeb=V(2, 160, 128), gupb=V(4, 32, 256),
        gus=V(4, 512, 256), gusi=V(4, 512, 256), gu=V(4, 4, 128, 256), gui=V(3, 4, 128, 256),
        guy=V(2, 4, 64, 256), guyi=V(4, 64, 256), guz=V(2, 4, 32, 256),
        gn=F(8, 128), rgz=F(7, 8, 128), rgy=F(3, 8, 128), rgx=F(3, 8, 128), rgc=F(8, 128), gns=F(3, 8, 128),
        kv_sem=pltpu.SemaphoreType.DMA((2,)),
        send_sem=pltpu.SemaphoreType.DMA((SENDS + 1,)),
        recv_sem=pltpu.SemaphoreType.DMA((RECVS,)),
    )

    def body(*refs):
        own = refs[:13]
        kernel(*own, **dict(zip(scratch, refs[13:])))

    gx, gup, glat, grope, ggain = pl.pallas_call(
        body,
        out_shape=(
            jax.ShapeDtypeStruct((128, 5120), bf16),
            jax.ShapeDtypeStruct((32, 2048), bf16),
            jax.ShapeDtypeStruct((32, 320), bf16),
            jax.ShapeDtypeStruct((4, 320), bf16),
            jax.ShapeDtypeStruct((1, 512), f32),
        ),
        in_specs=[pl.BlockSpec(memory_space=pl.ANY)] + [whole] * 5 + [pl.BlockSpec(memory_space=pl.ANY), whole],
        out_specs=(whole,) * 5,
        scratch_shapes=list(scratch.values()),
        compiler_params=pltpu.CompilerParams(
            collective_id=0, has_side_effects=True, vmem_limit_bytes=60 << 20
        ),
    )(
        inputs, latent, gain.reshape(1, 512), w_latent, w_rope.T, w_up,
        grad_kv.reshape(2, 8, 128, 2048), grad_rope.T,
    )

    def hand_over(*refs):
        for i in range(5):
            refs[5 + i][...] = refs[i][...]

    made = (gx, gup, glat, grope, ggain)
    gx, gup, glat, grope, ggain = pl.pallas_call(
        hand_over,
        out_shape=tuple(jax.ShapeDtypeStruct(a.shape, a.dtype) for a in made),
        in_specs=[whole] * 5,
        out_specs=(whole,) * 5,
    )(*made)
    return gx, gup, glat.T, grope.T, ggain.reshape(512)


def solution(mesh):
    in_specs = (
        P(("dp", "tensor"), None),
        P(("dp", "tensor"), None),
        P(),
        P("tensor", None),
        P("tensor", None),
        P("dp", "tensor"),
        P("dp", "tensor"),
        P(("dp", "tensor"), None),
    )
    out_specs = (
        P(("dp", "tensor"), None),
        P("dp", "tensor"),
        P("tensor", "dp"),
        P("tensor", "dp"),
        P(),
    )
    return jax.shard_map(shards, mesh=mesh, in_specs=in_specs, out_specs=out_specs, check_vma=False)
```

time: 139 us -> 118 us (0.85)
  local copies, waits for them, and re-layouts: 11.5 us -> 0 us
  Pallas kernels: 127 us -> 117 us
    pallas_call x1 -> x2, Pallas kernels: 127 us -> 117 us  [the longest x1 115 us: shards(): pl.pallas_call(body, out_shape=(jax.ShapeDtypeStruct((128, 5120), bf16),...]
    unnamed x9 -> x0, local copies, waits for them, and re-layouts: 5.8 us -> none
    transpose x2 -> x0, local copies, waits for them, and re-layouts: 1.86 us -> none  [the longest x1 1.76 us: shards(): grad_x = gx.transpose(1, 0, 2).reshape(128, 5120)]
    slice x2 -> x0, local copies, waits for them, and re-layouts: 1.51 us -> none  [the longest x1 0.79 us: shards(): glat[:, :, 0:32].reshape(2, 64, 128)]
where the time goes in v2:
time: 118 us
  Pallas kernels  117 us (99%)
    pallas_call x1, Pallas kernels, shards(): pl.pallas_call(body, out_shape=(jax.ShapeDtypeStruct((128, 5120), bf16),...  115 us
    pallas_call x1, Pallas kernels, shards(): pl.pallas_call(hand_over, out_shape=tuple((jax.ShapeDtypeStruct(a.shape,...  2.56 us

profile of v2, /device:TPU:1, one launch (start us, length us, event | category | flops | bytes accessed | tf_op | source)
XLA Modules:
  0.0 118.1 jit_solution(6406290472806242907)
XLA Ops:
  0.6 114.9 %shard_map.119 = (bf16[128,5120]{1,0:T(8,128)(2,1)}, bf16[32,2048]{1,0:T(8,128)(2,1)}, bf16[32,320]{1,0:T(8,128)(2,1)}, bf16[4,320]{1,0:T(4,128)(2,1)}, f32[1,512]{1,0:T(1,128)}) custom-call(bf16[128,5120]{1,0:T(8,128)(2,1)} %refs_0_.1, bf16[128,512]{1,0:T(8,128)(2,1)} %refs_1_.1, f32[1,512]{1,0:T(1,128)} %bitcast.10, bf16[320,512]{1,0:T(8,128)(2,1)} %refs_3_.1, ...), custom_call_target="tpu_custom_call" | custom-call | tf_op jit(solution)/shard_map/pallas_call | solution.py:772
  115.5 2.6 %shard_map.120 = (bf16[128,5120]{1,0:T(8,128)(2,1)}, bf16[32,2048]{1,0:T(8,128)(2,1)}, bf16[32,320]{1,0:T(8,128)(2,1)}, bf16[4,320]{1,0:T(4,128)(2,1)}, f32[1,512]{1,0:T(1,128)}) custom-call(bf16[128,5120]{1,0:T(8,128)(2,1)} %get-tuple-element.15.refs_0_, bf16[32,2048]{1,0:T(8,128)(2,1)} %get-tuple-element.16.refs_1_, ...), custom_call_target="tpu_custom_call" | custom-call | tf_op jit(solution)/shard_map/pallas_call | solution.py:797

commit v3 on v2

--- a/solution.py
+++ b/solution.py
@@ -368,12 +368,8 @@
             m.wait(ublock(p.at_x(-o), 1 - yh, 1 - c), usib[4 + o], sib)
 
     up_arrive(yh, -1, 3, 1, 2)
-    nb.arrive(2)
-    nb.forward(2)
-    nb_over(p.at_z(-2), 3)
-    nb_over(p.at_z(2), 4)
-    na.arrive(2)
-    na.forward(2)
+    wg.arrive(2)
+    wg.forward(2)
     load_kv.wait()
     m.wait(ublock(x, yh, 1 - c), usib[0], sib)
     m.wait(ublock(x, 1 - yh, 1 - c), usib[1], sib)
@@ -466,32 +462,29 @@
     lax.fori_loop(3, 5, more(0), 0)
     a0.step(2)
     a1s.step(2)
+    wg.arrive(3)
+    wg.forward(3)
+    wsend(-2, 2, -3, 3)
     lax.fori_loop(3, 8, more(1), 0)
     for k in range(3, 8):
         over(k)
     over_in(0)
     by.step(0)
     lax.fori_loop(5, 8, more(0), 0)
-    wg.arrive(2)
-    wg.forward(2)
-    wsend(-2, 2)
-    nb.arrive(3)
-    nb.forward(3)
-    nb_over(p.at_z(-3), 5)
-    nb_over(p.at_z(3), 6)
-    na.arrive(3)
-    na.forward(3)
     a0.step(3)
     a1s.step(3)
     over_in(1)
     over_in(2)
     by.step(1)
-    wg.arrive(3)
-    wg.forward(3)
-    wsend(-3, 3)
+    nb.arrive(2)
+    nb.forward(2)
+    nb_over(p.at_z(-2), 3)
+    nb_over(p.at_z(2), 4)
+    na.arrive(2)
+    na.forward(2)
+    wg.arrive(4)
+    wsend(4)
     rs.step(0)
-    nb.arrive(4)
-    nb_over(p.at_z(4), 7)
     over_in(3)
     over_in(4)
     by.step(2)
@@ -502,9 +495,6 @@
         m.send(gay_out.at[i, 1 - yl], gay_in.at[i], gay_slots[i], ylo)
         for h in range(2):
             part[0, h, :, 128 * i : 128 * i + 128] = half_a[h]
-    na.arrive(4)
-    wg.arrive(4)
-    wsend(4)
     rs.step(1)
     over_in(5)
     over_in(6)
@@ -512,6 +502,12 @@
     wonward(0, -1, 1)
     over_in(7)
     part[0, 0, :, 256:512] = by.last()
+    nb.arrive(3)
+    nb.forward(3)
+    nb_over(p.at_z(-3), 5)
+    nb_over(p.at_z(3), 6)
+    na.arrive(3)
+    na.forward(3)
     for i in range(2):
         m.wait(gay_in.at[i], gay_slots[i], ylo)
     own_a = part[0, yl, :, 0:256] + jnp.concatenate([gay_in[0], gay_in[1]], axis=1).astype(f32)
@@ -534,6 +530,9 @@
     for o in range(1, 8):
         m.send(gn, rgz.at[o - 1], rgz_slots[o - 1], p.dev_z(o))
 
+    nb.arrive(4)
+    nb_over(p.at_z(4), 7)
+    wonward(-2, 2, -3, 3, 4)
     m.wait(pres, pre_slot, sib)
     both = jnp.concatenate([pre[...], pres[...]], axis=0)
 
@@ -557,25 +556,28 @@
     r1_slots = [m.slot() for _ in range(3)]
     r2_slots = [m.slot() for _ in range(3)]
     for o in (2, 1, 3):
-        m.send(gw.at[p.at_x(o), :, pl.ds(0, 64)], r1.at[o - 1], r1_slots[o - 1], p.dev_x(o))
+        m.send(gw.at[p.at_x(o), :, pl.ds(0, 32)], r1.at[o - 1], r1_slots[o - 1], p.dev_x(o))
         hh, ll = p.at_y(o)
         m.send(
-            gw.at[:, pl.ds(8 * ll, 8), pl.ds(pl.multiple_of(64 + 32 * hh, 16), 32)],
+            gw.at[:, pl.ds(8 * ll, 8), pl.ds(pl.multiple_of(32 + 48 * hh, 16), 48)],
             r2.at[o - 1], r2_slots[o - 1], p.dev_y(o),
         )
 
+    na.arrive(4)
     for i, o in enumerate((0, -1, 1, -2, 2, -3, 3, 4)):
         nb_arrive(p.at_z(o), i)
-    lax.fori_loop(0, 4, theirs_tile, 0)
-    gus_slot = m.slot()
-    m.send(gus, gusi, gus_slot, sib)
-    m.wait(gusi, gus_slot, sib)
-    lax.fori_loop(0, 4, mine_tile, 0)
-    gux = [m.slot() for _ in range(3)]
-    for o in (1, 3, 2):
-        m.send(gu.at[p.at_x(o)], gui.at[o - 1], gux[o - 1], p.dev_x(o))
+    gus_slots = [m.slot() for _ in range(2)]
+    for h in range(2):
+        lax.fori_loop(2 * h, 2 * h + 2, theirs_tile, 0)
+        m.send(gus.at[pl.ds(2 * h, 2)], gusi.at[pl.ds(2 * h, 2)], gus_slots[h], sib)
+    gux = [m.slot() for _ in range(6)]
+    for h in range(2):
+        m.wait(gusi.at[pl.ds(2 * h, 2)], gus_slots[h], sib)
+        lax.fori_loop(2 * h, 2 * h + 2, mine_tile, 0)
+        for o in (1, 3, 2):
+            tiles = pl.ds(2 * h, 2)
+            m.send(gu.at[p.at_x(o), tiles], gui.at[o - 1, tiles], gux[3 * h + o - 1], p.dev_x(o))
     rs.step(2)
-    wonward(-2, 2, -3, 3, 4)
     rs.step(3)
     turned = rs.last().astype(bf16)
     for o in (1, 7, 2, 6, 3, 5, 4):
@@ -600,7 +602,7 @@
     for o in (1, 3, 2):
         m.wait(r1.at[o - 1], r1_slots[o - 1], p.dev_x(o))
     for h in range(2):
-        rows = pl.ds(32 * h, 32)
+        rows = pl.ds(16 * h, 16)
         sum1 = gw[x, :, rows].astype(f32)
         for o in range(3):
             sum1 = sum1 + r1[o, :, rows].astype(f32)
@@ -612,7 +614,7 @@
     for o in (1, 3, 2):
         m.wait(r2.at[o - 1], r2_slots[o - 1], p.dev_y(o))
     for q in range(4):
-        sum2 = gw[q, pl.ds(8 * yl, 8), pl.ds(pl.multiple_of(64 + 32 * yh, 16), 32)].astype(f32)
+        sum2 = gw[q, pl.ds(8 * yl, 8), pl.ds(pl.multiple_of(32 + 48 * yh, 16), 48)].astype(f32)
         for o in range(3):
             sum2 = sum2 + r2[o, q].astype(f32)
         a2[q] = sum2.astype(bf16)
@@ -658,19 +660,20 @@
     sum1 = a1[yh, pl.ds(8 * yl, 8)].astype(f32)
     for o in range(3):
         sum1 = sum1 + ry[o].astype(f32)
-    a12[:, 0:32] = sum1.astype(bf16)
+    a12[:, 0:16] = sum1.astype(bf16)
     for o in (1, 3, 2):
         m.wait(rx.at[o - 1], rx_slots[o - 1], p.dev_x(o))
     sum2 = a2[x].astype(f32)
     for o in range(3):
         sum2 = sum2 + rx[o].astype(f32)
-    a12[:, 32:64] = sum2.astype(bf16)
+    a12[:, 16:64] = sum2.astype(bf16)
     r12_slots = [m.slot() for _ in range(7)]
     for o in range(1, 8):
         m.send(a12.at[p.at_z(o)], r12.at[o - 1], r12_slots[o - 1], p.dev_z(o))
 
     for o in (1, 3, 2):
-        m.wait(gui.at[o - 1], gux[o - 1], p.dev_x(o))
+        for h in range(2):
+            m.wait(gui.at[o - 1, pl.ds(2 * h, 2)], gux[3 * h + o - 1], p.dev_x(o))
     for h in range(2):
         rows = pl.ds(64 * h, 64)
         total = gu[x, :, rows].astype(f32)
@@ -731,7 +734,7 @@
     m.wait(glatb.at[1 - c, 1 - yh], fin_slots[2], yhi_other)
     rows = []
     for h in range(2):
-        for lo, n in ((0, 32), (32, 32), (64, 16)):
+        for lo, n in ((0, 16), (16, 48), (64, 16)):
             for i in range(2):
                 rows.append(glatb[h, i, lo : lo + n])
     glat[...] = columns((p.dp % 4) * 32, 32, jnp.concatenate(rows, axis=0))
@@ -751,10 +754,10 @@
         gay_out=V(2, 2, 128, 128), gay_in=V(2, 128, 128), gnorm=F(128, 512),
         wx=V(320, 640), wq=V(8, 80, 640), wa=V(80, 640), wc=V(8, 320, 640), intr=V(2, 16, 160, 128), ins=V(16, 160, 128),
         pre=V(128, 640), pres=V(128, 640), gxs=V(128, 2560),
-        rp=V(128, 128), rps=V(128, 128), gw=V(4, 16, 128, 128), gw3=V(8, 4, 2, 32, 128), r1=V(3, 16, 64, 128), r2=V(3, 4, 8, 32, 128), r3z=V(7, 4, 2, 32, 128),
-        a1=V(2, 16, 32, 128), a2=V(4, 8, 32, 128),
+        rp=V(128, 128), rps=V(128, 128), gw=V(4, 16, 128, 128), gw3=V(8, 4, 2, 32, 128), r1=V(3, 16, 32, 128), r2=V(3, 4, 8, 48, 128), r3z=V(7, 4, 2, 32, 128),
+        a1=V(2, 16, 16, 128), a2=V(4, 8, 48, 128),
         s3=V(8, 160, 128), s3p=V(4, 160, 128), s3m=V(4, 160, 128),
-        a3x=V(4, 224, 128), r3x=V(3, 224, 128), ry=V(3, 8, 32, 128), rx=V(3, 8, 32, 128),
+        a3x=V(4, 224, 128), r3x=V(3, 224, 128), ry=V(3, 8, 16, 128), rx=V(3, 8, 48, 128),
         a12=V(8, 64, 128), r12=V(7, 64, 128), a3y=V(4, 176, 128), r3y=V(3, 176, 128),
         fin=V(80, 128), rfin=V(160, 128), glatb=V(2, 2, 80, 128), gropeb=V(2, 160, 128), gupb=V(4, 32, 256),
         gus=V(4, 512, 256), gusi=V(4, 512, 256), gu=V(4, 4, 128, 256), gui=V(3, 4, 128, 256),

time: 118 us -> 115 us (0.975)
  Pallas kernels: 117 us -> 115 us
    pallas_call x1, Pallas kernels: 115 us -> 112 us  [shards(): pl.pallas_call(body, out_shape=(jax.ShapeDtypeStruct((128, 5120), bf16),...]
where the time goes in v3:
time: 115 us
  Pallas kernels  115 us (100%)
    pallas_call x1, Pallas kernels, shards(): pl.pallas_call(body, out_shape=(jax.ShapeDtypeStruct((128, 5120), bf16),...  112 us
    pallas_call x1, Pallas kernels, shards(): pl.pallas_call(hand_over, out_shape=tuple((jax.ShapeDtypeStruct(a.shape,...  2.56 us

profile of v3, /device:TPU:1, one launch (start us, length us, event | category | flops | bytes accessed | tf_op | source)
XLA Modules:
  0.0 115.2 jit_solution(7244864571945121058)
XLA Ops:
  0.6 112.0 %shard_map.119 = (bf16[128,5120]{1,0:T(8,128)(2,1)}, bf16[32,2048]{1,0:T(8,128)(2,1)}, bf16[32,320]{1,0:T(8,128)(2,1)}, bf16[4,320]{1,0:T(4,128)(2,1)}, f32[1,512]{1,0:T(1,128)}) custom-call(bf16[128,5120]{1,0:T(8,128)(2,1)} %refs_0_.1, bf16[128,512]{1,0:T(8,128)(2,1)} %refs_1_.1, f32[1,512]{1,0:T(1,128)} %bitcast.10, bf16[320,512]{1,0:T(8,128)(2,1)} %refs_3_.1, ...), custom_call_target="tpu_custom_call" | custom-call | tf_op jit(solution)/shard_map/pallas_call | solution.py:775
  112.7 2.6 %shard_map.120 = (bf16[128,5120]{1,0:T(8,128)(2,1)}, bf16[32,2048]{1,0:T(8,128)(2,1)}, bf16[32,320]{1,0:T(8,128)(2,1)}, bf16[4,320]{1,0:T(4,128)(2,1)}, f32[1,512]{1,0:T(1,128)}) custom-call(bf16[128,5120]{1,0:T(8,128)(2,1)} %get-tuple-element.15.refs_0_, bf16[32,2048]{1,0:T(8,128)(2,1)} %get-tuple-element.16.refs_1_, ...), custom_call_target="tpu_custom_call" | custom-call | tf_op jit(solution)/shard_map/pallas_call | solution.py:800
